TPU v7x, 256 devices: a whole 4x4x8 slice. The times are simulated.
256 devices in a mesh: win: 64 (over z_hi, y, x), chan: 4 (over z_lo, core).
Axes of the slice: x: 4, y: 4, z: 8 (z_hi: 4, z_lo: 2; z = z_hi * 2 + z_lo), core: 2. Of those that a mesh axis runs over, the one named last changes fastest.
Arguments:
- records: float32 [1024, 2048, 256], P('win', 'chan'), may hold values from -6 to 6
- keep: int32 [1024], P('win'), may hold values 0 or 1
- pairs: int32 [4, 2], replicated, may hold values from 0 to 15
Outputs:
- correlations: float32 [4, 16384, 512], P('chan', 'win')
All inputs are finite; a program needn't handle non-finite values. No bound on the sum of `keep` on one device may be relied on, other than what follows from the above.
Results may differ from a plain program's by a relative error of at most 0.0075.
Values may be sent and summed in bfloat16 or wider, within the bound.
No kernel may reach another device: no remote copies, remote signals or barrier semaphores. Data moves between devices by JAX's collectives and lax.ppermute only.
A program may use at most 128 MiB of HBM per device.

v0:
```python
import math

import jax
import jax.numpy as jnp
from jax import lax
from jax.sharding import PartitionSpec as P

BLK = 128
NBAND = 128
PB_OWN = 1


def segment_taper(length):
    steps = jnp.arange(length, dtype=jnp.float32)
    return 0.5 - 0.5 * jnp.cos(2.0 * math.pi * (steps + 0.5) / length)


def forward_table(seg, nfft, nband):
    steps = jnp.arange(seg, dtype=jnp.int32)
    freqs = jnp.arange(1, nband + 1, dtype=jnp.int32)
    phase = (steps[:, None] * freqs[None, :] % nfft).astype(jnp.float32) * (2.0 * math.pi / nfft)
    scale = 1.0 / math.sqrt(seg)
    return (jnp.concatenate([jnp.cos(phase), -jnp.sin(phase)], axis=1) * scale).astype(jnp.bfloat16)


def inverse_table(nfft, nband):
    freqs = jnp.arange(1, nband + 1, dtype=jnp.int32)
    lagged = jnp.arange(nfft, dtype=jnp.int32) - nfft // 2
    phase = (freqs[:, None] * lagged[None, :] % nfft).astype(jnp.float32) * (2.0 * math.pi / nfft)
    return jnp.concatenate([jnp.cos(phase), -jnp.sin(phase)], axis=0).astype(jnp.bfloat16)


def prepare(records, keep):
    centred = records - jnp.mean(records, axis=2, keepdims=True)
    power = jnp.mean(centred * centred, axis=2, keepdims=True)
    weight = keep.astype(jnp.float32)[:, None, None]
    taper = segment_taper(records.shape[2])
    return (centred * lax.rsqrt(power + 1e-06) * taper * weight).astype(jnp.bfloat16)


def cross(left, right):
    half = left.shape[2] // 2
    lsplit = left.reshape(left.shape[0], left.shape[1], 2, half)
    rsplit = right.reshape(right.shape[0], right.shape[1], 2, half)
    turned = jnp.stack([lsplit[:, :, 1], -lsplit[:, :, 0]], axis=2)
    real = jnp.einsum("iscf,jscf->ijf", lsplit, rsplit, preferred_element_type=jnp.float32)
    imag = jnp.einsum("iscf,jscf->ijf", turned, rsplit, preferred_element_type=jnp.float32)
    return jnp.stack([real, imag], axis=2).reshape(left.shape[0] * right.shape[0], 2, half)


def shards(records, keep, pairs):
    seg = records.shape[2]
    prepared = prepare(records, keep)
    table = forward_table(seg, 2 * seg, NBAND)
    back = inverse_table(2 * seg, NBAND)
    total = records.shape[0] * lax.axis_size("win")
    scale = 1.0 / math.sqrt(total * NBAND)
    owner = lax.axis_index("chan")
    mine = lax.dynamic_slice_in_dim(pairs, owner * PB_OWN, PB_OWN, 0).reshape(-1)
    spectra = jnp.einsum("sct,tf->csf", prepared, table, preferred_element_type=jnp.float32).astype(
        jnp.bfloat16
    )
    whole = lax.all_gather(spectra, "chan", axis=0, tiled=True)
    rows = whole.reshape(-1, BLK, whole.shape[1], whole.shape[2])[mine]
    rows = rows.reshape(PB_OWN, 2, BLK, rows.shape[2], rows.shape[3])
    terms = jnp.stack([cross(rows[0, 0], rows[0, 1])])
    terms = terms.reshape(PB_OWN, BLK * BLK, 2 * NBAND)
    stacked = lax.psum_scatter(terms, "win", scatter_dimension=1, tiled=True).astype(jnp.bfloat16)
    lagged = jnp.einsum("pef,fl->pel", stacked, back, preferred_element_type=jnp.float32)
    return lagged * scale


def solution(mesh):
    in_specs = (P("win", "chan", None), P("win"), P())
    out_specs = P("chan", "win", None)
    return jax.shard_map(shards, mesh=mesh, in_specs=in_specs, out_specs=out_specs, check_vma=False)
```

profile of v0, /device:TPU:1, one launch (start us, length us, event | category | flops | bytes accessed | tf_op | source)
XLA Modules:
  0.0 700.7 jit_solution(1741187622229064243)
XLA Ops:
  6.6 0.6 fusion.29
  7.2 4.5 reduce_sum.18
  11.8 4.7 multiply_reduce_fusion
  16.5 6.5 convert_bitcast_fusion
  22.9 0.0 all-gather.2.cloned.1.call-update
  23.0 0.0 reduce-scatter.2.cloned.1.call-start
  23.0 0.2 dynamic-slice_reduce_fusion
  23.2 157.9 %all-gather.2.cloned.1.call-done = bf16[2048,16,256]{0,2,1:T(8,128)(2,1)} async-done(((bf16[512,16,256]{0,2,1:T(8,128)(2,1)}), bf16[2048,16,256]{0,2,1:T(8,128)(2,1)}) %all-gather.2.cloned.1.call-update) | async-done | bytes 16777232 | tf_op jit(solution)/shard_map/all_gather | solution.py:63
  181.1 15.1 %copy.15 = bf16[512,8,16,128]{3,2,1,0:T(8,128)(2,1)} copy(bf16[512,8,16,128]{3,1,2,0:T(8,128)(2,1)} %bitcast.42) | data formatting | bytes 33554432
  196.2 23.6 %copy.4 = bf16[16,128,16,256]{3,1,2,0:T(8,128)(2,1)} copy(bf16[16,128,16,256]{1,0,3,2:T(8,128)(2,1)} %bitcast.41) | data formatting | bytes 33554432 | tf_op jit(solution)/shard_map/reshape | solution.py:64
  219.8 6.4 gather_fusion
  226.2 1.1 fusion.36
  227.4 1.6 copy.6
  229.0 0.7 copy.8
  229.7 1.1 fusion.37
  230.8 0.7 copy.5
  231.5 1.5 convolution_bitcast_fusion.1
  233.0 1.3 convolution_bitcast_fusion
  234.3 6.0 pad_maximum_fusion
  240.3 17.5 %copy.12 = f32[128,128,2,128]{1,0,3,2:T(8,128)} copy(f32[128,128,2,128]{0,1,3,2:T(8,128)} %pad_maximum_fusion) | data formatting | bytes 33554432 | tf_op jit(solution)/shard_map/stack | solution.py:48
  257.8 18.2 %reshape_stack_reshape.3 = f32[1,16384,256]{1,2,0:T(8,128)} reshape(f32[128,128,2,128]{1,0,3,2:T(8,128)} %copy.12) | data formatting | bytes 33554432 | tf_op jit(solution)/shard_map/reshape;stack;reshape | solution.py:67
  276.1 1.2 cosine_convert_fusion
  277.3 414.5 %reduce-scatter.2.cloned.1.call-done = f32[1,256,256]{1,2,0:T(8,128)} async-done(((f32[1,16384,256]{1,2,0:T(8,128)}), f32[1,256,256]{1,2,0:T(8,128)}) %reduce-scatter.2.cloned.1.call-update) | async-done | bytes 262160 | tf_op jit(solution)/shard_map/reduce_scatter | solution.py:68
  691.8 2.0 fusion.5
  (20 shorter events, 0.1 us)
Async XLA Ops:
  6.5 16.5 %copy-start = (s32[4,2]{0,1:T(2,128)S(1)}, s32[4,2]{0,1:T(2,128)}, u32[]{:S(2)}) copy-start(s32[4,2]{0,1:T(2,128)} %param.5) | copy-start | bytes 100
  6.5 174.6 %all-gather.2.cloned.1.call-start = ((), (), s32[]{:S(2)}) async-start(), calls=%async_computation.1 | async-start | bytes 20971520 | tf_op jit(solution)/shard_map/all_gather | solution.py:63
  7.2 9.3 %copy-start.4 = (s32[16]{0:T(128)S(1)}, s32[16]{0:T(128)}, u32[]{:S(2)}) copy-start(s32[16]{0:T(128)} %param.4) | copy-start | bytes 196
  23.0 668.9 %reduce-scatter.2.cloned.1.call-start = ((), (), s32[]{:S(2)}) async-start(), calls=%async_computation.2 | async-start | bytes 17039360 | tf_op jit(solution)/shard_map/reduce_scatter | solution.py:68
  231.4 1.6 copy-start.2
  231.4 1.6 copy-start.3
  276.0 417.8 %copy-start.1 = (s32[4,2]{0,1:T(2,128)S(1)}, s32[4,2]{0,1:T(2,128)}, u32[]{:S(2)}) copy-start(s32[4,2]{0,1:T(2,128)} %param.5) | copy-start | bytes 100
Sparse Core Ops, SparseCore 0:
  23.1 157.9 all-gather.1
  276.2 415.5 reduce-scatter.1
where the time goes:
time: 713 us; the launch traced here: 701 us
  waiting for transfers between devices  572 us (80%)
  local copies, waits for them, and re-layouts  85.1 us (12%)
  other arithmetic  18.2 us (3%)
  between operations  13.6 us (2%)
  matrix products  11.3 us (2%)
    reduce_scatter x1, waiting for transfers between devices, shards(): lax.psum_scatter(terms, 'win', scatter_dimension=1, tiled=True)  414 us
    all_gather x1, waiting for transfers between devices, shards(): whole = lax.all_gather(spectra, 'chan', axis=0, tiled=True)  158 us
    reshape x1, local copies, waits for them, and re-layouts, shards(): rows = whole.reshape(-1, BLK, whole.shape[1], whole.shape[2])[mine]  23.6 us
    another operation x1, local copies, waits for them, and re-layouts, shards(): terms = terms.reshape(PB_OWN, BLK * BLK, 2 * NBAND)  18.2 us
    another operation x1, local copies, waits for them, and re-layouts, cross(): jnp.stack([real, imag], axis=2)  17.5 us
    unnamed x11, local copies, waits for them, and re-layouts  15.1 us
  transfers between devices with their start and end apart: 2, of which 2 were waited for; matrix products, arithmetic and copies ran while one was open for 0% of the time, Pallas kernels for 0%

commit v1 on v0

v1 whole, which is shorter than its diff:
```python
import math

import jax
import jax.numpy as jnp
import numpy as np
from jax import lax
from jax.experimental import pallas as pl
from jax.experimental.pallas import tpu as pltpu
from jax.sharding import Mesh
from jax.sharding import PartitionSpec as P

BLK = 128
NBAND = 128
SEG = 256
NFFT = 512
NPAIR = 4
ZH, YX, ZL, CORE = 4, 16, 2, 2
OWN_SEGS = 16
OWN_BLKS = 4
BINS = 2
F32, BF16 = jnp.float32, jnp.bfloat16
MIB = 1 << 20


def bins_of(half, quarter):
    first = (half * ZL + quarter) * YX * BINS
    return (1 + first + np.arange(YX * BINS)).reshape(YX, BINS)


def forward_rows(bins):
    phase = (bins.reshape(-1, 1) * np.arange(SEG)[None, :]) % NFFT
    angle = phase.astype(np.float64) * (2.0 * math.pi / NFFT)
    both = np.stack([np.cos(angle), -np.sin(angle)], axis=1)
    return (both.reshape(-1, SEG) / math.sqrt(SEG)).astype(np.float32)


def forward_tables():
    tables = []
    for zl in range(ZL):
        for core in range(CORE):
            rows = [
                forward_rows(bins_of(core ^ other_core, zl ^ other_z))
                for other_core in range(CORE)
                for other_z in range(ZL)
            ]
            tables.append(np.concatenate(rows))
    return np.stack(tables)


def inverse_rows():
    order = np.stack(
        [np.stack([bins_of(core, zl) for core in range(CORE)], axis=1) for zl in range(ZL)], axis=1
    )
    phase = (order.reshape(-1, 1) * (np.arange(NFFT)[None, :] - NFFT // 2)) % NFFT
    angle = phase.astype(np.float64) * (2.0 * math.pi / NFFT)
    both = np.stack([np.cos(angle), -np.sin(angle)], axis=1)
    return both.reshape(-1, 2 * BINS, NFFT).astype(np.float32)


def spectra_kernel(chan_ref, keep_ref, records_ref, table_ref, taper_ref, mine_ref, theirs_ref, rows_ref):
    table = table_ref[0]
    taper = taper_ref[...]
    for s in range(OWN_SEGS):
        samples = records_ref[s]
        centred = samples - jnp.mean(samples, axis=1, keepdims=True)
        power = jnp.mean(centred * centred, axis=1, keepdims=True)
        weight = keep_ref[s].astype(F32)
        prepared = (centred * lax.rsqrt(power + 1e-06) * taper * weight).astype(BF16)
        spectra = lax.dot_general(table, prepared, (((1,), (1,)), ((), ())), preferred_element_type=F32)
        rows_ref[pl.ds(s, 2 * NBAND, stride=OWN_SEGS), :] = spectra
    half = NBAND * OWN_SEGS
    shape = (ZL, 1, YX, 2 * BINS, OWN_SEGS, BLK)
    mine_ref[...] = rows_ref[:half, :].astype(BF16).reshape(shape)
    theirs_ref[...] = rows_ref[half:, :].astype(BF16).reshape(shape)


def spectra_of(records, keep, chan):
    tables = jnp.asarray(forward_tables(), BF16)
    steps = np.arange(SEG, dtype=np.float64)
    taper = jnp.asarray((0.5 - 0.5 * np.cos(2.0 * math.pi * (steps + 0.5) / SEG)).astype(np.float32)[None])
    out = jax.ShapeDtypeStruct((ZL, OWN_BLKS, YX, 2 * BINS, OWN_SEGS, BLK), BF16)
    out_spec = pl.BlockSpec((ZL, 1, YX, 2 * BINS, OWN_SEGS, BLK), lambda b, c, k: (0, b, 0, 0, 0, 0))
    return pl.pallas_call(
        spectra_kernel,
        grid_spec=pltpu.PrefetchScalarGridSpec(
            num_scalar_prefetch=2,
            grid=(OWN_BLKS,),
            in_specs=[
                pl.BlockSpec((OWN_SEGS, BLK, SEG), lambda b, c, k: (0, b, 0)),
                pl.BlockSpec((1, 2 * NBAND, SEG), lambda b, c, k: (c[0], 0, 0)),
                pl.BlockSpec((1, SEG), lambda b, c, k: (0, 0)),
            ],
            out_specs=[out_spec, out_spec],
            scratch_shapes=[pltpu.VMEM((2 * NBAND * OWN_SEGS, BLK), F32)],
        ),
        out_shape=[out, out],
        compiler_params=pltpu.CompilerParams(vmem_limit_bytes=32 * MIB),
        cost_estimate=pl.CostEstimate(flops=2 * 8192 * 256 * 256, bytes_accessed=13 * MIB, transcendentals=8192),
        name="spectra",
    )(chan, keep, records, tables, taper)


def whose(block, zl, core):
    return block // (CORE * OWN_BLKS) == zl, (block // OWN_BLKS) % CORE == core


def half_entry(ref, *at):
    return ref.at[at]


def sending_kernel(place_ref, pairs_ref, mine_ref, other_ref, inner_ref, outer_ref):
    zl, core = place_ref[0], place_ref[1]

    def take(block, bin_, d):
        _, own = whose(block, zl, core)
        slot = block % OWN_BLKS
        rows = pl.ds(bin_ * 2, 2)
        return jnp.where(own, mine_ref[1, slot, d, rows], other_ref[1, slot, d, rows])

    for p in range(NPAIR):
        a, b = pairs_ref[2 * p], pairs_ref[2 * p + 1]
        here_a, _ = whose(a, zl, core)
        here_b, _ = whose(b, zl, core)
        both = here_a & here_b
        first = jnp.where(here_a, a, b)
        second = jnp.where(both, b, first)
        second_bin = jnp.where(both, 0, 1)

        def step(d, carry, p=p, a=a, b=b, first=first, second=second, second_bin=second_bin):
            inner_ref[d, p, 0] = take(first, 0, d)
            inner_ref[d, p, 1] = take(second, second_bin, d)
            outer_ref[d, p, 0] = take(a, 1, d)
            outer_ref[d, p, 1] = take(b, 1, d)
            return carry

        lax.fori_loop(0, YX, step, 0)


def vmem():
    return pl.BlockSpec(memory_space=pltpu.VMEM)


def smem():
    return pl.BlockSpec(memory_space=pltpu.SMEM)


def sending(place, pairs, mine, other):
    out = jax.ShapeDtypeStruct((YX, NPAIR, 2, 2, OWN_SEGS, BLK), BF16)
    return pl.pallas_call(
        sending_kernel,
        in_specs=[smem(), smem(), vmem(), vmem()],
        out_specs=[vmem(), vmem()],
        out_shape=[out, out],
        compiler_params=pltpu.CompilerParams(vmem_limit_bytes=32 * MIB),
        cost_estimate=pl.CostEstimate(flops=0, bytes_accessed=4 * MIB, transcendentals=0),
        name="sending",
    )(place, pairs, mine, other)


def factors_kernel(place_ref, pairs_ref, mine_ref, other_ref, inner_ref, outer_ref, out_ref):
    zl, core = place_ref[0], place_ref[1]
    for p in range(NPAIR):
        blocks = (pairs_ref[2 * p], pairs_ref[2 * p + 1])
        here = [whose(block, zl, core)[0] for block in blocks]
        for side in range(2):
            block = blocks[side]
            own = whose(block, zl, core)[1]
            slot = block % OWN_BLKS
            lone = here[1 - side]

            def step(d, carry, p=p, side=side, own=own, slot=slot, lone=lone, is_here=here[side]):
                for bin_ in range(BINS):
                    rows = pl.ds(bin_ * 2, 2)
                    kept = jnp.where(own, mine_ref[0, slot, d, rows], other_ref[0, slot, d, rows])
                    apart = inner_ref[d, p, bin_]
                    together = inner_ref[d, p, side] if bin_ == 0 else outer_ref[d, p, side]
                    came = jnp.where(lone, apart, together)
                    out_ref[d, p, side, rows] = jnp.where(is_here, kept, came)
                return carry

            lax.fori_loop(0, YX, step, 0)


def factors(place, pairs, mine, other, inner, outer):
    return pl.pallas_call(
        factors_kernel,
        in_specs=[smem(), smem(), vmem(), vmem(), vmem(), vmem()],
        out_specs=vmem(),
        out_shape=jax.ShapeDtypeStruct((YX, NPAIR, 2, 2 * BINS, OWN_SEGS, BLK), BF16),
        compiler_params=pltpu.CompilerParams(vmem_limit_bytes=32 * MIB),
        cost_estimate=pl.CostEstimate(flops=0, bytes_accessed=6 * MIB, transcendentals=0),
        name="factors",
    )(place, pairs, mine, other, inner, outer)


def products_kernel(factors_ref, out_ref, part_ref, rows_ref):
    length = YX * OWN_SEGS
    for p in range(NPAIR):
        for bin_ in range(BINS):
            x, y = (
                jnp.concatenate(
                    [factors_ref[:, p, side, 2 * bin_ + c].reshape(length, BLK) for c in range(2)], axis=1
                )
                for side in range(2)
            )
            g = lax.dot_general(x, y, (((0,), (0,)), ((), ())), preferred_element_type=F32)
            part_ref[0] = g[:BLK, :BLK] + g[BLK:, BLK:]
            part_ref[1] = g[BLK:, :BLK] - g[:BLK, BLK:]
            for c in range(2):
                for r in range(2):
                    at = p * 8 + r * 4 + bin_ * 2 + c
                    rows_ref[pl.ds(at, BLK // 2, stride=8 * NPAIR), :] = part_ref[c, pl.ds(r, BLK // 2, stride=2), :]
    out_ref[...] = rows_ref[...].astype(BF16)


def products(gathered):
    return pl.pallas_call(
        products_kernel,
        in_specs=[vmem()],
        out_specs=vmem(),
        out_shape=jax.ShapeDtypeStruct((BLK // 2 * NPAIR * 8, BLK), BF16),
        scratch_shapes=[pltpu.VMEM((2, BLK, BLK), F32), pltpu.VMEM((BLK // 2 * NPAIR * 8, BLK), F32)],
        compiler_params=pltpu.CompilerParams(vmem_limit_bytes=32 * MIB),
        cost_estimate=pl.CostEstimate(flops=2 * 8 * 256**3, bytes_accessed=3 * MIB, transcendentals=0),
        name="products",
    )(gathered)


def lags_kernel(scale, shares_ref, back_ref, out_ref):
    total = shares_ref[0].astype(F32)
    for z in range(1, ZH):
        total += shares_ref[z].astype(F32)
    stacked = total.astype(BF16)
    for r in range(2):
        lagged = lax.dot_general(stacked, back_ref[r], (((0,), (0,)), ((), ())), preferred_element_type=F32)
        out_ref[0, r * BLK : (r + 1) * BLK, :] = lagged * scale


def lags(shares, total):
    rows = inverse_rows()
    back = np.zeros((2, rows.shape[0], 2, 2 * BINS, NFFT), np.float32)
    for r in range(2):
        back[r, :, r] = rows
    back = jnp.asarray(back.reshape(2, 4 * NBAND, NFFT), BF16)
    scale = 1.0 / math.sqrt(total * NBAND)
    return pl.pallas_call(
        lambda *refs: lags_kernel(scale, *refs),
        in_specs=[vmem(), vmem()],
        out_specs=vmem(),
        out_shape=jax.ShapeDtypeStruct((1, 2 * BLK, NFFT), F32),
        compiler_params=pltpu.CompilerParams(vmem_limit_bytes=32 * MIB),
        cost_estimate=pl.CostEstimate(flops=4 * 512 * 128 * 512, bytes_accessed=2 * MIB, transcendentals=0),
        name="lags",
    )(shares, back)


def shards(records, keep, pairs):
    zl, core = lax.axis_index("zl"), lax.axis_index("core")
    place = jnp.stack([zl, core]).astype(jnp.int32)
    chan = (zl * CORE + core).astype(jnp.int32).reshape(1)
    flat = pairs.reshape(-1)
    mine, theirs = spectra_of(records, keep, chan)
    other = lax.ppermute(theirs, "core", [(0, 1), (1, 0)])
    inner, outer = sending(place, flat, mine, other)
    inner = lax.ppermute(inner, "zl", [(0, 1), (1, 0)])
    turns = []
    for zh in range(ZH):
        turns.append((zh * ZL, (zh - 1) % ZH * ZL + 1))
        turns.append((zh * ZL + 1, (zh + 1) % ZH * ZL))
    outer = lax.ppermute(outer, ("zh", "zl"), turns)
    sides = factors(place, flat, mine, other, inner, outer)
    gathered = lax.all_to_all(sides, ("y", "x"), 0, 0, tiled=True)
    shares = products(gathered).reshape(ZH * YX * NPAIR, 8, BLK)
    shares = lax.all_to_all(shares, ("zh", "y", "x", "zl", "core"), 0, 0, tiled=True)
    total = records.shape[0] * ZH * YX
    return lags(shares.reshape(ZH, YX * NPAIR * 8, BLK), total)


def solution(mesh):
    fine = Mesh(mesh.devices.reshape(ZH, 4, 4, ZL, CORE), ("zh", "y", "x", "zl", "core"))
    win, chan = ("zh", "y", "x"), ("zl", "core")
    in_specs = (P(win, chan, None), P(win), P())
    out_specs = P(chan, win, None)
    return jax.shard_map(shards, mesh=fine, in_specs=in_specs, out_specs=out_specs, check_vma=False)
```

time: 713 us -> 124 us (0.17); the launches traced: 701 us -> 124 us
  waiting for transfers between devices: 572 us -> 26.8 us
  local copies, waits for them, and re-layouts: 85.1 us -> 5.94 us
  blocking collectives: 0 us -> 64 us
  Pallas kernels: 0 us -> 19 us
  other arithmetic: 18.2 us -> 0.07 us
  between operations: 13.6 us -> 0.04 us
  matrix products: 11.3 us -> 0 us
  starting transfers between devices: 0.04 us -> 7.89 us
    reduce_scatter x1 -> x0, waiting for transfers between devices: 414 us -> none  [shards(): lax.psum_scatter(terms, 'win', scatter_dimension=1, tiled=True)]
    all_gather x1 -> x0, waiting for transfers between devices: 158 us -> none  [shards(): whole = lax.all_gather(spectra, 'chan', axis=0, tiled=True)]
    all_to_all x0 -> x2, blocking collectives: none -> 64 us  [the longest x1 33.7 us: shards(): gathered = lax.all_to_all(sides, ('y', 'x'), 0, 0, tiled=True)]
    another operation x3 -> x0, local copies, waits for them, and re-layouts: 36.4 us -> none  [the longest x1 18.2 us: shards(): terms = terms.reshape(PB_OWN, BLK * BLK, 2 * NBAND)]
    ppermute x0 -> x3, waiting for transfers between devices: none -> 26.8 us  [the longest x1 19.8 us: shards(): inner = lax.ppermute(inner, 'zl', [(0, 1), (1, 0)])]
    reshape x1, local copies, waits for them, and re-layouts: 23.6 us -> 0.09 us  [shards(): flat = pairs.reshape(-1)]
    pallas_call x0 -> x5, Pallas kernels: none -> 19 us  [the longest x1 9.13 us: spectra_of(): pl.pallas_call(spectra_kernel, grid_spec=pltpu.PrefetchScalarGridSpec(num...]
    dot_general x4 -> x0, matrix products: 11.3 us -> none  [the longest x1 6.47 us: shards(): jnp.einsum('sct,tf->csf', prepared, table, preferred_element_type=jnp.flo...]
  transfers between devices with their start and end apart: 2 -> 3, of which waited for: 2 -> 3; matrix products, arithmetic and copies ran while one was open for 0% -> 0% of each run, Pallas kernels for 0% -> 0%
where the time goes in v1:
time: 124 us
  blocking collectives  64 us (52%)
  waiting for transfers between devices  26.8 us (22%)
  Pallas kernels  19 us (15%)
  starting transfers between devices  7.89 us (6%)
  local copies, waits for them, and re-layouts  5.94 us (5%)
    all_to_all x1, blocking collectives, shards(): gathered = lax.all_to_all(sides, ('y', 'x'), 0, 0, tiled=True)  33.7 us
    all_to_all x1, blocking collectives, shards(): lax.all_to_all(shares, ('zh', 'y', 'x', 'zl', 'core'), 0, 0, tiled=True)  30.4 us
    ppermute x1, waiting for transfers between devices, shards(): inner = lax.ppermute(inner, 'zl', [(0, 1), (1, 0)])  19.8 us
    pallas_call x1, Pallas kernels, spectra_of(): pl.pallas_call(spectra_kernel, grid_spec=pltpu.PrefetchScalarGridSpec(num...  9.13 us
    unnamed x13, local copies, waits for them, and re-layouts  5.85 us
    pallas_call x1, Pallas kernels, sending(): pl.pallas_call(sending_kernel, in_specs=[smem(), smem(), vmem(), vmem()],...  4.59 us
    ppermute x1, starting transfers between devices, shards(): outer = lax.ppermute(outer, ('zh', 'zl'), turns)  4.55 us
    ppermute x1, waiting for transfers between devices, shards(): other = lax.ppermute(theirs, 'core', [(0, 1), (1, 0)])  3.87 us
  transfers between devices with their start and end apart: 3, of which 3 were waited for; matrix products, arithmetic and copies ran while one was open for 0% of the time, Pallas kernels for 0%

profile of v1, /device:TPU:1, one launch (start us, length us, event | category | flops | bytes accessed | tf_op | source)
XLA Modules:
  0.0 123.8 jit_solution(3918329151526767268)
XLA Ops:
  0.0 0.0 copy-start
  0.0 3.4 %copy-done = f32[16,512,256]{2,1,0:T(8,128)S(1)} copy-done((f32[16,512,256]{2,1,0:T(8,128)S(1)}, f32[16,512,256]{2,1,0:T(8,128)}, u32[]{:S(2)}) %copy-start) | copy-done | bytes 8388632
  3.4 0.0 copy-start.2
  3.4 1.0 copy-done.2
  4.4 0.7 copy-done.3
  5.1 0.7 copy-done.4
  5.8 9.1 %spectra.1 = (bf16[2,4,16,4,16,128]{5,4,3,2,1,0:T(8,128)(2,1)S(1)}, bf16[2,4,16,4,16,128]{5,4,3,2,1,0:T(8,128)(2,1)}) custom-call(s32[1]{0:T(128)} %bitcast.2.chan_ref, s32[16]{0:T(128)S(1)} %copy-done.4, f32[16,512,256]{2,1,0:T(8,128)S(1)} %copy-done, bf16[4,256,256]{2,1,0:T(8,128)(2,1)S(1)} %copy-done.2, f32[1,256]{1,0:T(1,128)S(1)} %copy-done.3), custom_call_target="tpu_custom_call" | custom-call | flops 1073741824 | bytes 13631488 | tf_op jit(solution)/shard_map/spectra/pallas_call | solution.py:83
  14.9 3.2 %collective-permute-start = (bf16[2,4,16,4,16,128]{5,4,3,2,1,0:T(8,128)(2,1)}, bf16[2,4,16,4,16,128]{5,4,3,2,1,0:T(8,128)(2,1)}, u32[]{:S(2)}, u32[]{:S(2)}) collective-permute-start(bf16[2,4,16,4,16,128]{5,4,3,2,1,0:T(8,128)(2,1)} %get-tuple-element.10), channel_id=1, source_target_pairs={{0,1},{1,0},{2,3},{3,2},{4,5},{5,4},{6,7},{7,6},{8,9},{9,8},{10,11... | collective-permute-start | bytes 6291464 | tf_op jit(solution)/shard_map/ppermute | solution.py:263
  18.1 0.0 copy-done.5
  18.1 0.1 copy.8
  18.2 0.1 reshape.12.pairs_ref
  18.3 0.1 pad_add_fusion.place_ref
  18.4 3.9 %collective-permute-done.other_ref = bf16[2,4,16,4,16,128]{5,4,3,2,1,0:T(8,128)(2,1)} collective-permute-done((bf16[2,4,16,4,16,128]{5,4,3,2,1,0:T(8,128)(2,1)}, bf16[2,4,16,4,16,128]{5,4,3,2,1,0:T(8,128)(2,1)}, u32[]{:S(2)}, u32[]{:S(2)}) %collective-permute-start) | collective-permute-done | bytes 2097184 | tf_op jit(solution)/shard_map/ppermute | solution.py:263
  22.3 4.6 %sending.1 = (bf16[16,4,2,2,16,128]{5,4,3,2,1,0:T(8,128)(2,1)S(1)}, bf16[16,4,2,2,16,128]{5,4,3,2,1,0:T(8,128)(2,1)S(1)}) custom-call(s32[2]{0:T(128)S(1)} %pad_add_fusion.place_ref, s32[8]{0:T(128)S(1)} %reshape.12.pairs_ref, bf16[2,4,16,4,16,128]{5,4,3,2,1,0:T(8,128)(2,1)S(1)} %get-tuple-element.9.mine_ref, ...), custom_call_target="tpu_custom_call" | custom-call | bytes 4194304 | tf_op jit(solution)/shard_map/sending/pallas_call | solution.py:149
  26.9 0.1 collective-permute-start.1
  27.0 4.6 %collective-permute-start.2 = (bf16[16,4,2,2,16,128]{5,4,3,2,1,0:T(8,128)(2,1)S(1)}, bf16[16,4,2,2,16,128]{5,4,3,2,1,0:T(8,128)(2,1)S(1)}, u32[]{:S(2)}, u32[]{:S(2)}) collective-permute-start(bf16[16,4,2,2,16,128]{5,4,3,2,1,0:T(8,128)(2,1)S(1)} %get-tuple-element.12), channel_id=1, source_target_pairs={{0,194},{2,64},{64,2},{66,128},{128,66},{130,192},{192,130},{194,0... | collective-permute-start | bytes 3145736 | tf_op jit(solution)/shard_map/ppermute | solution.py:270
  31.5 19.8 %collective-permute-done.1.inner_ref = bf16[16,4,2,2,16,128]{5,4,3,2,1,0:T(8,128)(2,1)S(1)} collective-permute-done((bf16[16,4,2,2,16,128]{5,4,3,2,1,0:T(8,128)(2,1)S(1)}, bf16[16,4,2,2,16,128]{5,4,3,2,1,0:T(8,128)(2,1)S(1)}, u32[]{:S(2)}, u32[]{:S(2)}) %collective-permute-start.1) | collective-permute-done | bytes 1048608 | tf_op jit(solution)/shard_map/ppermute | solution.py:265
  51.3 3.1 %collective-permute-done.2.outer_ref = bf16[16,4,2,2,16,128]{5,4,3,2,1,0:T(8,128)(2,1)S(1)} collective-permute-done((bf16[16,4,2,2,16,128]{5,4,3,2,1,0:T(8,128)(2,1)S(1)}, bf16[16,4,2,2,16,128]{5,4,3,2,1,0:T(8,128)(2,1)S(1)}, u32[]{:S(2)}, u32[]{:S(2)}) %collective-permute-start.2) | collective-permute-done | bytes 1048608 | tf_op jit(solution)/shard_map/ppermute | solution.py:270
  54.4 3.1 %factors.1 = bf16[16,4,2,4,16,128]{5,4,3,2,1,0:T(8,128)(2,1)S(1)} custom-call(s32[2]{0:T(128)S(1)} %pad_add_fusion.place_ref, s32[8]{0:T(128)S(1)} %reshape.12.pairs_ref, bf16[2,4,16,4,16,128]{5,4,3,2,1,0:T(8,128)(2,1)S(1)} %get-tuple-element.9.mine_ref, bf16[2,4,16,4,16,128]{5,4,3,2,1,0:T(8,128)(2,1)} %collective-permute-done.other_ref, ...), custom_call_target="tpu_custom_call" | custom-call | bytes 6291456 | tf_op jit(solution)/shard_map/factors/pallas_call | solution.py:185
  57.5 33.7 %all_to_all.10.factors_ref = bf16[16,4,2,4,16,128]{5,4,3,2,1,0:T(8,128)(2,1)S(1)} all-to-all(bf16[16,4,2,4,16,128]{5,4,3,2,1,0:T(8,128)(2,1)S(1)} %factors.1), channel_id=1, replica_groups=mesh['zh'=4,'y'=4,'x'=4,'zl'=2,'core'=2] {'y','x'}, dimensions={0} | all-to-all | bytes 4194304 | tf_op jit(solution)/shard_map/all_to_all | solution.py:272
  91.2 1.1 products.1
  92.3 30.4 %all_to_all.11 = bf16[256,8,128]{2,1,0:T(8,128)(2,1)S(1)} all-to-all(bf16[256,8,128]{2,1,0:T(8,128)(2,1)S(1)} %bitcast.5), channel_id=1, replica_groups=mesh['zh'=4,'y'=4,'x'=4,'zl'=2,'core'=2] {'zh','y','x','zl','core'}, dimensions={0} | all-to-all | bytes 1048576 | tf_op jit(solution)/shard_map/all_to_all | solution.py:274
  122.6 0.0 copy-done.1
  122.6 1.1 lags.1
  (4 shorter events, 0.0 us)
Async XLA Ops:
  0.0 3.4 %copy-start = (f32[16,512,256]{2,1,0:T(8,128)S(1)}, f32[16,512,256]{2,1,0:T(8,128)}, u32[]{:S(2)}) copy-start(f32[16,512,256]{2,1,0:T(8,128)} %records_ref.1) | copy-start | bytes 25165828
  3.4 1.0 copy-start.2
  4.4 0.7 copy-start.3
  5.1 0.7 copy-start.4
  5.8 12.4 %copy-start.5 = (s32[4,2]{0,1:T(2,128)S(1)}, s32[4,2]{0,1:T(2,128)}, u32[]{:S(2)}) copy-start(s32[4,2]{0,1:T(2,128)} %param.8) | copy-start | bytes 100
  14.9 7.4 %collective-permute-start = (bf16[2,4,16,4,16,128]{5,4,3,2,1,0:T(8,128)(2,1)}, bf16[2,4,16,4,16,128]{5,4,3,2,1,0:T(8,128)(2,1)}, u32[]{:S(2)}, u32[]{:S(2)}) collective-permute-start(bf16[2,4,16,4,16,128]{5,4,3,2,1,0:T(8,128)(2,1)} %get-tuple-element.10), channel_id=1, source_target_pairs={{0,1},{1,0},{2,3},{3,2},{4,5},{5,4},{6,7},{7,6},{8,9},{9,8},{10,11... | collective-permute-start | bytes 6291464 | tf_op jit(solution)/shard_map/ppermute | solution.py:263
  26.9 24.5 %collective-permute-start.1 = (bf16[16,4,2,2,16,128]{5,4,3,2,1,0:T(8,128)(2,1)S(1)}, bf16[16,4,2,2,16,128]{5,4,3,2,1,0:T(8,128)(2,1)S(1)}, u32[]{:S(2)}, u32[]{:S(2)}) collective-permute-start(bf16[16,4,2,2,16,128]{5,4,3,2,1,0:T(8,128)(2,1)S(1)} %get-tuple-element.11), channel_id=1, source_target_pairs={{0,2},{2,0},{1,3},{3,1},{4,6},{6,4},{5,7},{7,5},{8,10},{10,8},{9,1... | collective-permute-start | bytes 3145736 | tf_op jit(solution)/shard_map/ppermute | solution.py:265
  27.0 27.5 %collective-permute-start.2 = (bf16[16,4,2,2,16,128]{5,4,3,2,1,0:T(8,128)(2,1)S(1)}, bf16[16,4,2,2,16,128]{5,4,3,2,1,0:T(8,128)(2,1)S(1)}, u32[]{:S(2)}, u32[]{:S(2)}) collective-permute-start(bf16[16,4,2,2,16,128]{5,4,3,2,1,0:T(8,128)(2,1)S(1)} %get-tuple-element.12), channel_id=1, source_target_pairs={{0,194},{2,64},{64,2},{66,128},{128,66},{130,192},{192,130},{194,0... | collective-permute-start | bytes 3145736 | tf_op jit(solution)/shard_map/ppermute | solution.py:270
  91.2 31.4 %copy-start.1 = (bf16[2,512,512]{2,1,0:T(8,128)(2,1)S(1)}, bf16[2,512,512]{2,1,0:T(8,128)(2,1)}, u32[]{:S(2)}) copy-start(bf16[2,512,512]{2,1,0:T(8,128)(2,1)} %constant.16.clone.refs_1_) | copy-start | bytes 3145732

commit v2 on v1

v2 whole, which is shorter than its diff:
```python
import math

import jax
import jax.numpy as jnp
import numpy as np
from jax import lax
from jax.experimental import pallas as pl
from jax.experimental.pallas import tpu as pltpu
from jax.sharding import Mesh
from jax.sharding import PartitionSpec as P

BLK = 128
NBAND = 128
SEG = 256
NFFT = 512
NPAIR = 4
ZH, YX, ZL, CORE = 4, 16, 2, 2
OWN_SEGS = 16
OWN_BLKS = 4
BINS = 2
F32, BF16 = jnp.float32, jnp.bfloat16
MIB = 1 << 20


def bins_of(half, quarter):
    first = (half * ZL + quarter) * YX * BINS
    return (1 + first + np.arange(YX * BINS)).reshape(YX, BINS)


def forward_rows(bins):
    phase = (bins.reshape(-1, 1) * np.arange(SEG)[None, :]) % NFFT
    angle = phase.astype(np.float64) * (2.0 * math.pi / NFFT)
    both = np.stack([np.cos(angle), -np.sin(angle)], axis=1)
    return (both.reshape(-1, SEG) / math.sqrt(SEG)).astype(np.float32)


def forward_tables():
    tables = []
    for zl in range(ZL):
        for core in range(CORE):
            near = [bins_of(0, zl), bins_of(1, zl)]
            far = [bins_of(core, zl ^ 1), bins_of(core ^ 1, zl ^ 1)]
            tables.append(np.concatenate([forward_rows(bins) for bins in near + far]))
    return np.stack(tables)


def inverse_rows():
    order = np.stack(
        [np.stack([bins_of(core, zl) for core in range(CORE)], axis=1) for zl in range(ZL)], axis=1
    )
    phase = (order.reshape(-1, 1) * (np.arange(NFFT)[None, :] - NFFT // 2)) % NFFT
    angle = phase.astype(np.float64) * (2.0 * math.pi / NFFT)
    both = np.stack([np.cos(angle), -np.sin(angle)], axis=1)
    return both.reshape(-1, 2 * BINS, NFFT).astype(np.float32)


def spectra_kernel(chan_ref, keep_ref, records_ref, table_ref, taper_ref, *refs):
    outs, rows_ref = refs[:-1], refs[-1]
    table = table_ref[0]
    taper = taper_ref[...]
    for s in range(OWN_SEGS):
        samples = records_ref[s]
        centred = samples - jnp.mean(samples, axis=1, keepdims=True)
        power = jnp.mean(centred * centred, axis=1, keepdims=True)
        weight = keep_ref[s].astype(F32)
        prepared = (centred * (lax.rsqrt(power + 1e-06) * weight) * taper).astype(BF16)
        spectra = lax.dot_general(table, prepared, (((1,), (1,)), ((), ())), preferred_element_type=F32)
        rows_ref[pl.ds(s, NBAND, stride=OWN_SEGS), :] = spectra
    length = NBAND * OWN_SEGS // len(outs)
    for n, out_ref in enumerate(outs):
        part = rows_ref[n * length : (n + 1) * length, :]
        out_ref[...] = part.astype(BF16).reshape(out_ref.shape)


def in_hbm(x):
    return pltpu.with_memory_space_constraint(x, pltpu.HBM)


def spectra(half, lead, count, name, chan, keep, records, tables):
    steps = np.arange(SEG, dtype=np.float64)
    taper = jnp.asarray((0.5 - 0.5 * np.cos(2.0 * math.pi * (steps + 0.5) / SEG)).astype(np.float32)[None])
    tail = (YX, 2 * BINS, OWN_SEGS, BLK)
    out = jax.ShapeDtypeStruct(lead + (OWN_BLKS,) + tail, BF16)
    out_spec = pl.BlockSpec(lead + (1,) + tail, lambda b, *_: (0,) * len(lead) + (b, 0, 0, 0, 0))
    return pl.pallas_call(
        spectra_kernel,
        grid_spec=pltpu.PrefetchScalarGridSpec(
            num_scalar_prefetch=2,
            grid=(OWN_BLKS,),
            in_specs=[
                pl.BlockSpec((OWN_SEGS, BLK, SEG), lambda b, *_: (0, b, 0)),
                pl.BlockSpec((1, NBAND, SEG), lambda b, c, k: (c[0], half, 0)),
                pl.BlockSpec((1, SEG), lambda b, *_: (0, 0)),
            ],
            out_specs=[out_spec] * count,
            scratch_shapes=[pltpu.VMEM((NBAND * OWN_SEGS, BLK), F32)],
        ),
        out_shape=[out] * count,
        compiler_params=pltpu.CompilerParams(vmem_limit_bytes=16 * MIB),
        cost_estimate=pl.CostEstimate(flops=8192 * 256 * 256, bytes_accessed=11 * MIB, transcendentals=8192),
        name=name,
    )(chan, keep, records, tables, in_hbm(taper))


def whose(block, zl, core):
    return block // (CORE * OWN_BLKS) == zl, (block // OWN_BLKS) % CORE == core


def vmem():
    return pl.BlockSpec(memory_space=pltpu.VMEM)


def smem():
    return pl.BlockSpec(memory_space=pltpu.SMEM)


def hbm():
    return pl.BlockSpec(memory_space=pltpu.HBM)


def copy_either(first, one, two, to, sem):
    @pl.when(first)
    def _():
        pltpu.make_async_copy(one, to, sem).start()

    @pl.when(jnp.logical_not(first))
    def _():
        pltpu.make_async_copy(two, to, sem).start()


def rows_of(bin_):
    return pl.ds(bin_ * 2, 2)


def sending_kernel(place_ref, pairs_ref, mine_ref, other_ref, inner_ref, outer_ref, sems):
    zl, core = place_ref[0], place_ref[1]
    copies = []

    def take(block, bin_, to):
        own = whose(block, zl, core)[1]
        at = (block % OWN_BLKS, slice(None), rows_of(bin_))
        sem = sems.at[len(copies)]
        copy_either(own, mine_ref.at[at], other_ref.at[at], to, sem)
        copies.append(pltpu.make_async_copy(mine_ref.at[at], to, sem))

    for p in range(NPAIR):
        a, b = pairs_ref[2 * p], pairs_ref[2 * p + 1]
        here_a, here_b = whose(a, zl, core)[0], whose(b, zl, core)[0]
        both = here_a & here_b
        first = jnp.where(here_a, a, b)
        take(first, 0, inner_ref.at[:, p, 0])
        take(jnp.where(both, b, first), jnp.where(both, 0, 1), inner_ref.at[:, p, 1])
        take(a, 1, outer_ref.at[:, p, 0])
        take(b, 1, outer_ref.at[:, p, 1])
    for copy in copies:
        copy.wait()


def sending(place, pairs, mine, other):
    out = jax.ShapeDtypeStruct((YX, NPAIR, 2, 2, OWN_SEGS, BLK), BF16)
    return pl.pallas_call(
        sending_kernel,
        in_specs=[smem(), smem(), hbm(), hbm()],
        out_specs=[hbm(), hbm()],
        out_shape=[out, out],
        scratch_shapes=[pltpu.SemaphoreType.DMA((4 * NPAIR,))],
        compiler_params=pltpu.CompilerParams(vmem_limit_bytes=4 * MIB),
        cost_estimate=pl.CostEstimate(flops=0, bytes_accessed=4 * MIB, transcendentals=0),
        name="sending",
    )(place, pairs, mine, other)


def places(pairs_ref, zl, core):
    for p in range(NPAIR):
        blocks = (pairs_ref[2 * p], pairs_ref[2 * p + 1])
        here = [whose(block, zl, core)[0] for block in blocks]
        for side in range(2):
            for bin_ in range(BINS):
                number = (2 * p + side) * BINS + bin_
                yield number, p, side, bin_, blocks[side], here[side], here[1 - side]


def kept_kernel(place_ref, pairs_ref, chip_ref, out_ref, sems):
    zl, core = place_ref[0], place_ref[1]
    for start in (True, False):
        for number, p, side, bin_, block, here, _ in places(pairs_ref, zl, core):
            at = (block % (CORE * OWN_BLKS), slice(None), rows_of(bin_))
            copy = pltpu.make_async_copy(chip_ref.at[at], out_ref.at[:, p, side, rows_of(bin_)], sems.at[number])

            @pl.when(here)
            def _(start=start, copy=copy):
                if start:
                    copy.start()
                else:
                    copy.wait()


def came_kernel(place_ref, pairs_ref, inner_ref, outer_ref, kept_ref, out_ref, sems):
    zl, core = place_ref[0], place_ref[1]
    for start in (True, False):
        for number, p, side, bin_, _, here, lone in places(pairs_ref, zl, core):
            to = out_ref.at[:, p, side, rows_of(bin_)]
            sem = sems.at[number]
            together = (inner_ref if bin_ == 0 else outer_ref).at[:, p, side]

            @pl.when(jnp.logical_not(here))
            def _(start=start, lone=lone, together=together, to=to, sem=sem, p=p, bin_=bin_):
                if start:
                    copy_either(lone, inner_ref.at[:, p, bin_], together, to, sem)
                else:
                    pltpu.make_async_copy(together, to, sem).wait()


def sides_of(kernel, name, place, pairs, *arrays):
    return pl.pallas_call(
        kernel,
        in_specs=[smem(), smem()] + [hbm()] * len(arrays),
        out_specs=hbm(),
        out_shape=jax.ShapeDtypeStruct((YX, NPAIR, 2, 2 * BINS, OWN_SEGS, BLK), BF16),
        scratch_shapes=[pltpu.SemaphoreType.DMA((2 * NPAIR * BINS,))],
        input_output_aliases={4: 0} if len(arrays) == 3 else {},
        compiler_params=pltpu.CompilerParams(vmem_limit_bytes=4 * MIB),
        cost_estimate=pl.CostEstimate(flops=0, bytes_accessed=3 * MIB, transcendentals=0),
        name=name,
    )(place, pairs, *arrays)


def products_kernel(factors_ref, out_ref, part_ref, rows_ref):
    length = YX * OWN_SEGS
    for p in range(NPAIR):
        for bin_ in range(BINS):
            x, y = (
                jnp.concatenate(
                    [factors_ref[:, p, side, 2 * bin_ + c].reshape(length, BLK) for c in range(2)], axis=1
                )
                for side in range(2)
            )
            g = lax.dot_general(x, y, (((0,), (0,)), ((), ())), preferred_element_type=F32)
            part_ref[0] = g[:BLK, :BLK] + g[BLK:, BLK:]
            part_ref[1] = g[BLK:, :BLK] - g[:BLK, BLK:]
            for c in range(2):
                for r in range(2):
                    at = p * 8 + r * 4 + bin_ * 2 + c
                    rows_ref[pl.ds(at, BLK // 2, stride=8 * NPAIR), :] = part_ref[c, pl.ds(r, BLK // 2, stride=2), :]
    out_ref[...] = rows_ref[...].astype(BF16)


def products(gathered):
    return pl.pallas_call(
        products_kernel,
        in_specs=[vmem()],
        out_specs=vmem(),
        out_shape=jax.ShapeDtypeStruct((BLK // 2 * NPAIR * 8, BLK), BF16),
        scratch_shapes=[pltpu.VMEM((2, BLK, BLK), F32), pltpu.VMEM((BLK // 2 * NPAIR * 8, BLK), F32)],
        compiler_params=pltpu.CompilerParams(vmem_limit_bytes=16 * MIB),
        cost_estimate=pl.CostEstimate(flops=2 * 8 * 256**3, bytes_accessed=3 * MIB, transcendentals=0),
        name="products",
    )(gathered)


def lags_kernel(scale, shares_ref, back_ref, out_ref):
    total = shares_ref[0].astype(F32)
    for z in range(1, ZH):
        total += shares_ref[z].astype(F32)
    stacked = total.astype(BF16)
    for r in range(2):
        lagged = lax.dot_general(stacked, back_ref[r], (((0,), (0,)), ((), ())), preferred_element_type=F32)
        out_ref[0, r * BLK : (r + 1) * BLK, :] = lagged * scale


def lags(shares, total):
    rows = inverse_rows()
    back = np.zeros((2, rows.shape[0], 2, 2 * BINS, NFFT), np.float32)
    for r in range(2):
        back[r, :, r] = rows
    back = jnp.asarray(back.reshape(2, 4 * NBAND, NFFT), BF16)
    scale = 1.0 / math.sqrt(total * NBAND)
    return pl.pallas_call(
        lambda *refs: lags_kernel(scale, *refs),
        in_specs=[vmem(), vmem()],
        out_specs=vmem(),
        out_shape=jax.ShapeDtypeStruct((1, 2 * BLK, NFFT), F32),
        compiler_params=pltpu.CompilerParams(vmem_limit_bytes=16 * MIB),
        cost_estimate=pl.CostEstimate(flops=4 * 512 * 128 * 512, bytes_accessed=2 * MIB, transcendentals=0),
        name="lags",
    )(shares, back)


def swap(x, axis):
    return lax.ppermute(x, axis, [(0, 1), (1, 0)])


def swap_outer(x):
    turns = []
    for zh in range(ZH):
        turns.append((zh * ZL, (zh - 1) % ZH * ZL + 1))
        turns.append((zh * ZL + 1, (zh + 1) % ZH * ZL))
    return lax.ppermute(x, ("zh", "zl"), turns)


def shards(records, keep, pairs):
    zl, core = lax.axis_index("zl"), lax.axis_index("core")
    place = jnp.stack([zl, core]).astype(jnp.int32)
    chan = (zl * CORE + core).astype(jnp.int32).reshape(1)
    flat = pairs.reshape(-1)
    tables = in_hbm(jnp.asarray(forward_tables(), BF16))
    records = in_hbm(records)
    mine_far, theirs_far = spectra(1, (), 2, "spectra_far", chan, keep, records, tables)
    other_far = swap(theirs_far, "core")
    inner, outer = sending(place, flat, mine_far, other_far)
    later, *_ = lax.optimization_barrier((chan, inner))
    inner, outer = swap(inner, "zl"), swap_outer(outer)
    (chip,) = spectra(0, (CORE,), 1, "spectra_near", later, keep, records, tables)
    chip = lax.all_to_all(chip, "core", 0, 0, tiled=True)
    chip = chip.reshape((CORE * OWN_BLKS,) + chip.shape[2:])
    kept = sides_of(kept_kernel, "kept", place, flat, chip)
    sides = sides_of(came_kernel, "came", place, flat, inner, outer, kept)
    gathered = lax.all_to_all(sides, ("y", "x"), 0, 0, tiled=True)
    shares = products(gathered).reshape(ZH * YX * NPAIR, 8, BLK)
    shares = lax.all_to_all(shares, ("zh", "y", "x", "zl", "core"), 0, 0, tiled=True)
    total = records.shape[0] * ZH * YX
    return lags(shares.reshape(ZH, YX * NPAIR * 8, BLK), total)


def solution(mesh):
    fine = Mesh(mesh.devices.reshape(ZH, 4, 4, ZL, CORE), ("zh", "y", "x", "zl", "core"))
    win, chan = ("zh", "y", "x"), ("zl", "core")
    in_specs = (P(win, chan, None), P(win), P())
    out_specs = P(chan, win, None)
    return jax.shard_map(shards, mesh=fine, in_specs=in_specs, out_specs=out_specs, check_vma=False)
```

time: 124 us -> 110 us (0.89)
  waiting for transfers between devices: 26.8 us -> 11.9 us
  local copies, waits for them, and re-layouts: 5.94 us -> 0.85 us
  blocking collectives: 64 us -> 68.9 us
  Pallas kernels: 19 us -> 20.3 us
    ppermute x3, waiting for transfers between devices: 26.8 us -> 11.9 us  [the longest x1 9.08 us: swap_outer(): return lax.ppermute(x, ('zh', 'zl'), turns)]
    all_to_all x0 -> x1, blocking collectives: none -> 5.7 us  [shards(): chip = lax.all_to_all(chip, 'core', 0, 0, tiled=True)]
    unnamed x13 -> x9, local copies, waits for them, and re-layouts: 5.85 us -> 0.76 us
    pallas_call x3 -> x5, Pallas kernels: 16.8 us -> 18.1 us  [the longest x2 14.8 us: spectra(): pl.pallas_call(spectra_kernel, grid_spec=pltpu.PrefetchScalarGridSpec(num...]
  transfers between devices with their start and end apart: 3 -> 3, of which waited for: 3 -> 3; matrix products, arithmetic and copies ran while one was open for 0% -> 0% of each run, Pallas kernels for 0% -> 8%
where the time goes in v2:
time: 110 us; the launch traced here: 109 us
  blocking collectives  68.9 us (63%)
  Pallas kernels  20.3 us (18%)
  waiting for transfers between devices  11.9 us (11%)
  starting transfers between devices  7.26 us (7%)
    all_to_all x1, blocking collectives, shards(): gathered = lax.all_to_all(sides, ('y', 'x'), 0, 0, tiled=True)  33.4 us
    all_to_all x1, blocking collectives, shards(): lax.all_to_all(shares, ('zh', 'y', 'x', 'zl', 'core'), 0, 0, tiled=True)  29.9 us
    pallas_call x2, Pallas kernels, spectra(): pl.pallas_call(spectra_kernel, grid_spec=pltpu.PrefetchScalarGridSpec(num...  14.8 us
    ppermute x1, waiting for transfers between devices, swap_outer(): return lax.ppermute(x, ('zh', 'zl'), turns)  9.08 us
    all_to_all x1, blocking collectives, shards(): chip = lax.all_to_all(chip, 'core', 0, 0, tiled=True)  5.7 us
    ppermute x1, starting transfers between devices, swap_outer(): return lax.ppermute(x, ('zh', 'zl'), turns)  3.92 us
    ppermute x2, starting transfers between devices, swap(): return lax.ppermute(x, axis, [(0, 1), (1, 0)])  3.33 us
    ppermute x2, waiting for transfers between devices, swap(): return lax.ppermute(x, axis, [(0, 1), (1, 0)])  2.85 us
  transfers between devices with their start and end apart: 3, of which 3 were waited for; matrix products, arithmetic and copies ran while one was open for 0% of the time, Pallas kernels for 8%

profile of v2, /device:TPU:1, one launch (start us, length us, event | category | flops | bytes accessed | tf_op | source)
XLA Modules:
  0.0 109.4 jit_solution(7952351409759945658)
XLA Ops:
  0.0 0.7 copy-done.1
  0.7 7.3 %spectra_far.1 = (bf16[4,16,4,16,128]{4,3,2,1,0:T(8,128)(2,1)S(1)}, bf16[4,16,4,16,128]{4,3,2,1,0:T(8,128)(2,1)S(1)}) custom-call(s32[1]{0:T(128)} %bitcast.2.chan_ref, s32[16]{0:T(128)S(1)} %copy-done.1, f32[16,512,256]{2,1,0:T(8,128)} %records_ref.3, bf16[4,256,256]{2,1,0:T(8,128)(2,1)} %constant.14.clone.table_ref, f32[1,256]{1,0:T(1,128)} %constant.15.clone.taper_ref), custom_call_target="tpu_custom_call" | custom-call | flops 536870912 | bytes 11534336 | tf_op jit(solution)/shard_map/spectra_far/pallas_call | solution.py:85
  8.0 0.0 copy-start.2
  8.0 3.3 %collective-permute-start = (bf16[4,16,4,16,128]{4,3,2,1,0:T(8,128)(2,1)S(1)}, bf16[4,16,4,16,128]{4,3,2,1,0:T(8,128)(2,1)S(1)}, u32[]{:S(2)}, u32[]{:S(2)}) collective-permute-start(bf16[4,16,4,16,128]{4,3,2,1,0:T(8,128)(2,1)S(1)} %get-tuple-element.11), channel_id=1, source_target_pairs={{0,1},{1,0},{2,3},{3,2},{4,5},{5,4},{6,7},{7,6},{8,9},{9,8},{10,11... | collective-permute-start | bytes 3145736 | tf_op jit(solution)/shard_map/ppermute | solution.py:290
  11.3 0.0 copy-done.3
  11.3 0.1 copy.10
  11.4 0.1 reshape.15.pairs_ref
  11.5 0.1 pad_add_fusion.place_ref
  11.6 2.0 %collective-permute-done.other_ref = bf16[4,16,4,16,128]{4,3,2,1,0:T(8,128)(2,1)S(1)} collective-permute-done((bf16[4,16,4,16,128]{4,3,2,1,0:T(8,128)(2,1)S(1)}, bf16[4,16,4,16,128]{4,3,2,1,0:T(8,128)(2,1)S(1)}, u32[]{:S(2)}, u32[]{:S(2)}) %collective-permute-start) | collective-permute-done | bytes 1048608 | tf_op jit(solution)/shard_map/ppermute | solution.py:290
  13.6 1.3 %sending.1 = (bf16[16,4,2,2,16,128]{5,4,3,2,1,0:T(8,128)(2,1)S(1)}, bf16[16,4,2,2,16,128]{5,4,3,2,1,0:T(8,128)(2,1)S(1)}) custom-call(s32[2]{0:T(128)S(1)} %pad_add_fusion.place_ref, s32[8]{0:T(128)S(1)} %reshape.15.pairs_ref, bf16[4,16,4,16,128]{4,3,2,1,0:T(8,128)(2,1)S(1)} %get-tuple-element.10.mine_ref, ...), custom_call_target="tpu_custom_call" | custom-call | bytes 4194304 | tf_op jit(solution)/shard_map/sending/pallas_call | solution.py:161
  15.0 3.9 %collective-permute-start.2 = (bf16[16,4,2,2,16,128]{5,4,3,2,1,0:T(8,128)(2,1)S(1)}, bf16[16,4,2,2,16,128]{5,4,3,2,1,0:T(8,128)(2,1)S(1)}, u32[]{:S(2)}, u32[]{:S(2)}) collective-permute-start(bf16[16,4,2,2,16,128]{5,4,3,2,1,0:T(8,128)(2,1)S(1)} %get-tuple-element.13), channel_id=1, source_target_pairs={{0,194},{2,64},{64,2},{66,128},{128,66},{130,192},{192,130},{194,0... | collective-permute-start | bytes 3145736 | tf_op jit(solution)/shard_map/ppermute | solution.py:298
  18.9 0.0 collective-permute-start.1
  18.9 0.0 copy-done.2
  18.9 7.4 %spectra_near.1 = bf16[2,4,16,4,16,128]{5,4,3,2,1,0:T(8,128)(2,1)S(1)} custom-call(s32[1]{0:T(128)} %bitcast.2.chan_ref, s32[16]{0:T(128)S(1)} %copy-done.2, f32[16,512,256]{2,1,0:T(8,128)} %records_ref.3, bf16[4,256,256]{2,1,0:T(8,128)(2,1)} %constant.14.clone.table_ref, f32[1,256]{1,0:T(1,128)} %constant.15.clone.taper_ref), custom_call_target="tpu_custom_call" | custom-call | flops 536870912 | bytes 11534336 | tf_op jit(solution)/shard_map/spectra_near/pallas_call | solution.py:85
  26.4 5.7 %all_to_all.15 = bf16[2,4,16,4,16,128]{5,4,3,2,1,0:T(8,128)(2,1)S(1)} all-to-all(bf16[2,4,16,4,16,128]{5,4,3,2,1,0:T(8,128)(2,1)S(1)} %spectra_near.1), channel_id=1, replica_groups=mesh['zh'=4,'y'=4,'x'=4,'zl'=2,'core'=2] {'core'}, dimensions={0} | all-to-all | bytes 4194304 | tf_op jit(solution)/shard_map/all_to_all | solution.py:314
  32.1 1.0 kept.1.kept_ref
  33.0 9.1 %collective-permute-done.2.outer_ref = bf16[16,4,2,2,16,128]{5,4,3,2,1,0:T(8,128)(2,1)S(1)} collective-permute-done((bf16[16,4,2,2,16,128]{5,4,3,2,1,0:T(8,128)(2,1)S(1)}, bf16[16,4,2,2,16,128]{5,4,3,2,1,0:T(8,128)(2,1)S(1)}, u32[]{:S(2)}, u32[]{:S(2)}) %collective-permute-start.2) | collective-permute-done | bytes 1048608 | tf_op jit(solution)/shard_map/ppermute | solution.py:298
  42.1 0.8 collective-permute-done.1.inner_ref
  43.0 1.0 came.1
  44.0 33.4 %all_to_all.16.factors_ref = bf16[16,4,2,4,16,128]{5,4,3,2,1,0:T(8,128)(2,1)S(1)} all-to-all(bf16[16,4,2,4,16,128]{5,4,3,2,1,0:T(8,128)(2,1)S(1)} %came.1), channel_id=1, replica_groups=mesh['zh'=4,'y'=4,'x'=4,'zl'=2,'core'=2] {'y','x'}, dimensions={0} | all-to-all | bytes 4194304 | tf_op jit(solution)/shard_map/all_to_all | solution.py:318
  77.4 1.1 products.1
  78.4 29.9 %all_to_all.17 = bf16[256,8,128]{2,1,0:T(8,128)(2,1)S(1)} all-to-all(bf16[256,8,128]{2,1,0:T(8,128)(2,1)S(1)} %bitcast.7), channel_id=1, replica_groups=mesh['zh'=4,'y'=4,'x'=4,'zl'=2,'core'=2] {'zh','y','x','zl','core'}, dimensions={0} | all-to-all | bytes 1048576 | tf_op jit(solution)/shard_map/all_to_all | solution.py:320
  108.3 0.0 copy-done
  108.3 1.1 %lags.1 = f32[1,256,512]{2,1,0:T(8,128)} custom-call(bf16[4,512,128]{2,1,0:T(8,128)(2,1)S(1)} %bitcast.8, bf16[2,512,512]{2,1,0:T(8,128)(2,1)S(1)} %copy-done), custom_call_target="tpu_custom_call" | custom-call | flops 134217728 | bytes 2097152 | tf_op jit(solution)/shard_map/lags/pallas_call | solution.py:278
  (3 shorter events, 0.0 us)
Async XLA Ops:
  0.0 0.7 copy-start.1
  0.7 10.7 %copy-start.3 = (s32[4,2]{0,1:T(2,128)S(1)}, s32[4,2]{0,1:T(2,128)}, u32[]{:S(2)}) copy-start(s32[4,2]{0,1:T(2,128)} %param.9) | copy-start | bytes 100
  8.0 10.9 %copy-start.2 = (s32[16]{0:T(128)S(1)}, s32[16]{0:T(128)}, u32[]{:S(2)}) copy-start(s32[16]{0:T(128)} %keep_ref.3) | copy-start | bytes 196
  8.0 5.6 %collective-permute-start = (bf16[4,16,4,16,128]{4,3,2,1,0:T(8,128)(2,1)S(1)}, bf16[4,16,4,16,128]{4,3,2,1,0:T(8,128)(2,1)S(1)}, u32[]{:S(2)}, u32[]{:S(2)}) collective-permute-start(bf16[4,16,4,16,128]{4,3,2,1,0:T(8,128)(2,1)S(1)} %get-tuple-element.11), channel_id=1, source_target_pairs={{0,1},{1,0},{2,3},{3,2},{4,5},{5,4},{6,7},{7,6},{8,9},{9,8},{10,11... | collective-permute-start | bytes 3145736 | tf_op jit(solution)/shard_map/ppermute | solution.py:290
  15.0 27.2 %collective-permute-start.2 = (bf16[16,4,2,2,16,128]{5,4,3,2,1,0:T(8,128)(2,1)S(1)}, bf16[16,4,2,2,16,128]{5,4,3,2,1,0:T(8,128)(2,1)S(1)}, u32[]{:S(2)}, u32[]{:S(2)}) collective-permute-start(bf16[16,4,2,2,16,128]{5,4,3,2,1,0:T(8,128)(2,1)S(1)} %get-tuple-element.13), channel_id=1, source_target_pairs={{0,194},{2,64},{64,2},{66,128},{128,66},{130,192},{192,130},{194,0... | collective-permute-start | bytes 3145736 | tf_op jit(solution)/shard_map/ppermute | solution.py:298
  18.9 24.0 %collective-permute-start.1 = (bf16[16,4,2,2,16,128]{5,4,3,2,1,0:T(8,128)(2,1)S(1)}, bf16[16,4,2,2,16,128]{5,4,3,2,1,0:T(8,128)(2,1)S(1)}, u32[]{:S(2)}, u32[]{:S(2)}) collective-permute-start(bf16[16,4,2,2,16,128]{5,4,3,2,1,0:T(8,128)(2,1)S(1)} %get-tuple-element.12), channel_id=1, source_target_pairs={{0,2},{2,0},{1,3},{3,1},{4,6},{6,4},{5,7},{7,5},{8,10},{10,8},{9,1... | collective-permute-start | bytes 3145736 | tf_op jit(solution)/shard_map/ppermute | solution.py:290
  77.4 30.9 %copy-start = (bf16[2,512,512]{2,1,0:T(8,128)(2,1)S(1)}, bf16[2,512,512]{2,1,0:T(8,128)(2,1)}, u32[]{:S(2)}) copy-start(bf16[2,512,512]{2,1,0:T(8,128)(2,1)} %constant.16.clone.refs_1_) | copy-start | bytes 3145732

commit v3 on v2

--- a/solution.py
+++ b/solution.py
@@ -1,3 +1,4 @@
+import functools
 import math
 
 import jax
@@ -18,6 +19,7 @@
 OWN_SEGS = 16
 OWN_BLKS = 4
 BINS = 2
+LEAST = 2
 F32, BF16 = jnp.float32, jnp.bfloat16
 MIB = 1 << 20
 
@@ -99,7 +101,7 @@
         compiler_params=pltpu.CompilerParams(vmem_limit_bytes=16 * MIB),
         cost_estimate=pl.CostEstimate(flops=8192 * 256 * 256, bytes_accessed=11 * MIB, transcendentals=8192),
         name=name,
-    )(chan, keep, records, tables, in_hbm(taper))
+    )(chan, keep, in_hbm(records), in_hbm(tables), in_hbm(taper))
 
 
 def whose(block, zl, core):
@@ -132,38 +134,94 @@
     return pl.ds(bin_ * 2, 2)
 
 
+def crossing(pairs, zl):
+    flags = []
+    alone, doubles = jnp.int32(0), jnp.int32(0)
+    for p in range(NPAIR):
+        a, b = (pairs[2 * p + side] // (CORE * OWN_BLKS) == zl for side in range(2))
+        one, both = jnp.where(a != b, 1, 0), jnp.where(a & b, 1, 0)
+        flags.append((one, both))
+        alone, doubles = alone + one, doubles + 2 * both
+    moved = jnp.maximum(doubles - alone, 0) // 2
+    inner, outer, seen = jnp.int32(0), jnp.int32(0), jnp.int32(0)
+    plan = []
+    for one, both in flags:
+        at = inner
+        inner = inner + one
+        bins = []
+        for _ in range(BINS):
+            near = seen < moved
+            bins.append((near, jnp.where(near, inner, outer)))
+            inner = inner + jnp.where(near, both, 0)
+            outer = outer + jnp.where(near, 0, both)
+            seen = seen + both
+        plan.append((one == 1, at, both == 1, bins))
+    return inner, outer, plan
+
+
+def couples_kernel(pairs_ref, out_ref):
+    most = jnp.int32(LEAST)
+    for zl in range(ZL):
+        inner, outer, _ = crossing(pairs_ref, zl)
+        most = jnp.maximum(most, jnp.maximum(inner, outer))
+    out_ref[0] = most
+
+
+def couples_of(pairs):
+    return pl.pallas_call(
+        couples_kernel,
+        in_specs=[smem()],
+        out_specs=smem(),
+        out_shape=jax.ShapeDtypeStruct((1,), jnp.int32),
+        name="couples",
+    )(pairs)[0]
+
+
 def sending_kernel(place_ref, pairs_ref, mine_ref, other_ref, inner_ref, outer_ref, sems):
     zl, core = place_ref[0], place_ref[1]
-    copies = []
-
-    def take(block, bin_, to):
-        own = whose(block, zl, core)[1]
-        at = (block % OWN_BLKS, slice(None), rows_of(bin_))
-        sem = sems.at[len(copies)]
-        copy_either(own, mine_ref.at[at], other_ref.at[at], to, sem)
-        copies.append(pltpu.make_async_copy(mine_ref.at[at], to, sem))
-
-    for p in range(NPAIR):
-        a, b = pairs_ref[2 * p], pairs_ref[2 * p + 1]
-        here_a, here_b = whose(a, zl, core)[0], whose(b, zl, core)[0]
-        both = here_a & here_b
-        first = jnp.where(here_a, a, b)
-        take(first, 0, inner_ref.at[:, p, 0])
-        take(jnp.where(both, b, first), jnp.where(both, 0, 1), inner_ref.at[:, p, 1])
-        take(a, 1, outer_ref.at[:, p, 0])
-        take(b, 1, outer_ref.at[:, p, 1])
-    for copy in copies:
-        copy.wait()
-
-
-def sending(place, pairs, mine, other):
-    out = jax.ShapeDtypeStruct((YX, NPAIR, 2, 2, OWN_SEGS, BLK), BF16)
+    plan = crossing(pairs_ref, zl)[2]
+    for start in (True, False):
+        for p in range(NPAIR):
+            blocks = (pairs_ref[2 * p], pairs_ref[2 * p + 1])
+            one, at, both, bins = plan[p]
+            here_a = whose(blocks[0], zl, core)[0]
+            lone = jnp.where(here_a, blocks[0], blocks[1])
+
+            def move(block, bin_, to, sem, start=start):
+                own = whose(block, zl, core)[1]
+                source = (block % OWN_BLKS, slice(None), rows_of(bin_))
+                if start:
+                    copy_either(own, mine_ref.at[source], other_ref.at[source], to, sem)
+                else:
+                    pltpu.make_async_copy(mine_ref.at[source], to, sem).wait()
+
+            for bin_ in range(BINS):
+                near, slot = bins[bin_]
+                number = (p * BINS + bin_) * 2
+
+                @pl.when(one)
+                def _(lone=lone, bin_=bin_, at=at, number=number, move=move):
+                    move(lone, bin_, inner_ref.at[at, bin_], sems.at[number])
+
+                for side in range(2):
+
+                    @pl.when(both & near)
+                    def _(block=blocks[side], bin_=bin_, slot=slot, side=side, number=number, move=move):
+                        move(block, bin_, inner_ref.at[slot, side], sems.at[number + side])
+
+                    @pl.when(both & jnp.logical_not(near))
+                    def _(block=blocks[side], bin_=bin_, slot=slot, side=side, number=number, move=move):
+                        move(block, bin_, outer_ref.at[slot, side], sems.at[number + side])
+
+
+def sending(couples, place, pairs, mine, other):
+    out = jax.ShapeDtypeStruct((couples, 2, YX, 2, OWN_SEGS, BLK), BF16)
     return pl.pallas_call(
         sending_kernel,
         in_specs=[smem(), smem(), hbm(), hbm()],
         out_specs=[hbm(), hbm()],
         out_shape=[out, out],
-        scratch_shapes=[pltpu.SemaphoreType.DMA((4 * NPAIR,))],
+        scratch_shapes=[pltpu.SemaphoreType.DMA((NPAIR * BINS * 2,))],
         compiler_params=pltpu.CompilerParams(vmem_limit_bytes=4 * MIB),
         cost_estimate=pl.CostEstimate(flops=0, bytes_accessed=4 * MIB, transcendentals=0),
         name="sending",
@@ -172,18 +230,16 @@
 
 def places(pairs_ref, zl, core):
     for p in range(NPAIR):
-        blocks = (pairs_ref[2 * p], pairs_ref[2 * p + 1])
-        here = [whose(block, zl, core)[0] for block in blocks]
         for side in range(2):
+            block = pairs_ref[2 * p + side]
             for bin_ in range(BINS):
-                number = (2 * p + side) * BINS + bin_
-                yield number, p, side, bin_, blocks[side], here[side], here[1 - side]
+                yield (2 * p + side) * BINS + bin_, p, side, bin_, block, whose(block, zl, core)[0]
 
 
 def kept_kernel(place_ref, pairs_ref, chip_ref, out_ref, sems):
     zl, core = place_ref[0], place_ref[1]
     for start in (True, False):
-        for number, p, side, bin_, block, here, _ in places(pairs_ref, zl, core):
+        for number, p, side, bin_, block, here in places(pairs_ref, zl, core):
             at = (block % (CORE * OWN_BLKS), slice(None), rows_of(bin_))
             copy = pltpu.make_async_copy(chip_ref.at[at], out_ref.at[:, p, side, rows_of(bin_)], sems.at[number])
 
@@ -197,18 +253,31 @@
 
 def came_kernel(place_ref, pairs_ref, inner_ref, outer_ref, kept_ref, out_ref, sems):
     zl, core = place_ref[0], place_ref[1]
+    plan = crossing(pairs_ref, 1 - zl)[2]
     for start in (True, False):
-        for number, p, side, bin_, _, here, lone in places(pairs_ref, zl, core):
+        for number, p, side, bin_, _, here in places(pairs_ref, zl, core):
+            one, at, both, bins = plan[p]
+            near, slot = bins[bin_]
             to = out_ref.at[:, p, side, rows_of(bin_)]
-            sem = sems.at[number]
-            together = (inner_ref if bin_ == 0 else outer_ref).at[:, p, side]
-
-            @pl.when(jnp.logical_not(here))
-            def _(start=start, lone=lone, together=together, to=to, sem=sem, p=p, bin_=bin_):
+
+            def move(source, to=to, sem=sems.at[number], start=start):
+                copy = pltpu.make_async_copy(source, to, sem)
                 if start:
-                    copy_either(lone, inner_ref.at[:, p, bin_], together, to, sem)
+                    copy.start()
                 else:
-                    pltpu.make_async_copy(together, to, sem).wait()
+                    copy.wait()
+
+            @pl.when(one & jnp.logical_not(here))
+            def _(move=move, at=at, bin_=bin_):
+                move(inner_ref.at[at, bin_])
+
+            @pl.when(both & near)
+            def _(move=move, slot=slot, side=side):
+                move(inner_ref.at[slot, side])
+
+            @pl.when(both & jnp.logical_not(near))
+            def _(move=move, slot=slot, side=side):
+                move(outer_ref.at[slot, side])
 
 
 def sides_of(kernel, name, place, pairs, *arrays):
@@ -298,23 +367,30 @@
     return lax.ppermute(x, ("zh", "zl"), turns)
 
 
+def both_sides(couples, place, pairs, chan, keep, records, tables, mine_far, other_far):
+    inner, outer = sending(couples, place, pairs, mine_far, other_far)
+    later, *_ = lax.optimization_barrier((chan, inner))
+    inner, outer = swap(inner, "zl"), swap_outer(outer)
+    (chip,) = spectra(0, (CORE,), 1, "spectra_near", later, keep, records, tables)
+    chip = lax.all_to_all(chip, "core", 0, 0, tiled=True)
+    chip = chip.reshape((CORE * OWN_BLKS,) + chip.shape[2:])
+    kept = sides_of(kept_kernel, "kept", place, pairs, chip)
+    return sides_of(came_kernel, "came", place, pairs, inner, outer, kept)
+
+
 def shards(records, keep, pairs):
     zl, core = lax.axis_index("zl"), lax.axis_index("core")
     place = jnp.stack([zl, core]).astype(jnp.int32)
     chan = (zl * CORE + core).astype(jnp.int32).reshape(1)
     flat = pairs.reshape(-1)
-    tables = in_hbm(jnp.asarray(forward_tables(), BF16))
-    records = in_hbm(records)
+    tables = jnp.asarray(forward_tables(), BF16)
     mine_far, theirs_far = spectra(1, (), 2, "spectra_far", chan, keep, records, tables)
     other_far = swap(theirs_far, "core")
-    inner, outer = sending(place, flat, mine_far, other_far)
-    later, *_ = lax.optimization_barrier((chan, inner))
-    inner, outer = swap(inner, "zl"), swap_outer(outer)
-    (chip,) = spectra(0, (CORE,), 1, "spectra_near", later, keep, records, tables)
-    chip = lax.all_to_all(chip, "core", 0, 0, tiled=True)
-    chip = chip.reshape((CORE * OWN_BLKS,) + chip.shape[2:])
-    kept = sides_of(kept_kernel, "kept", place, flat, chip)
-    sides = sides_of(came_kernel, "came", place, flat, inner, outer, kept)
+    sides = lax.switch(
+        couples_of(flat) - LEAST,
+        [functools.partial(both_sides, couples) for couples in range(LEAST, NPAIR + 1)],
+        *(place, flat, chan, keep, records, tables, mine_far, other_far),
+    )
     gathered = lax.all_to_all(sides, ("y", "x"), 0, 0, tiled=True)
     shares = products(gathered).reshape(ZH * YX * NPAIR, 8, BLK)
     shares = lax.all_to_all(shares, ("zh", "y", "x", "zl", "core"), 0, 0, tiled=True)

time: 110 us -> 103 us (0.936)
  waiting for transfers between devices: 11.9 us -> 0.2 us
  Pallas kernels: 20.3 us -> 23.3 us
    ppermute x1, waiting for transfers between devices: 9.08 us -> 0.01 us  [swap_outer(): return lax.ppermute(x, ('zh', 'zl'), turns)]
    ppermute x2, waiting for transfers between devices: 2.85 us -> 0.19 us  [swap(): return lax.ppermute(x, axis, [(0, 1), (1, 0)])]
    pallas_call x2, Pallas kernels: 2 us -> 3.51 us  [sides_of(): pl.pallas_call(kernel, in_specs=[smem(), smem()] + [hbm()] * len(arrays),...]
    pallas_call x0 -> x1, Pallas kernels: none -> 1.18 us  [couples_of(): pl.pallas_call(couples_kernel, in_specs=[smem()], out_specs=smem(), out_s...]
  transfers between devices with their start and end apart: 3 -> 3, of which waited for: 3 -> 1; matrix products, arithmetic and copies ran while one was open for 0% -> 0% of each run, Pallas kernels for 8% -> 10%
where the time goes in v3:
time: 103 us; the launch traced here: 101 us
  blocking collectives  69.3 us (67%)
  Pallas kernels  23.3 us (23%)
  starting transfers between devices  7.25 us (7%)
    all_to_all x1, blocking collectives, shards(): gathered = lax.all_to_all(sides, ('y', 'x'), 0, 0, tiled=True)  34.3 us
    all_to_all x1, blocking collectives, shards(): lax.all_to_all(shares, ('zh', 'y', 'x', 'zl', 'core'), 0, 0, tiled=True)  29.3 us
    pallas_call x2, Pallas kernels, spectra(): pl.pallas_call(spectra_kernel, grid_spec=pltpu.PrefetchScalarGridSpec(num...  15 us
    all_to_all x1, blocking collectives, both_sides(): chip = lax.all_to_all(chip, 'core', 0, 0, tiled=True)  5.69 us
    ppermute x1, starting transfers between devices, swap_outer(): return lax.ppermute(x, ('zh', 'zl'), turns)  3.92 us
    pallas_call x2, Pallas kernels, sides_of(): pl.pallas_call(kernel, in_specs=[smem(), smem()] + [hbm()] * len(arrays),...  3.51 us
    ppermute x2, starting transfers between devices, swap(): return lax.ppermute(x, axis, [(0, 1), (1, 0)])  3.33 us
  transfers between devices with their start and end apart: 3, of which 1 were waited for; matrix products, arithmetic and copies ran while one was open for 0% of the time, Pallas kernels for 10%

profile of v3, /device:TPU:1, one launch (start us, length us, event | category | flops | bytes accessed | tf_op | source)
XLA Modules:
  0.0 101.3 jit_solution(10714744114438937234)
XLA Ops:
  0.0 7.6 %spectra_far.1 = (bf16[4,16,4,16,128]{4,3,2,1,0:T(8,128)(2,1)S(1)}, bf16[4,16,4,16,128]{4,3,2,1,0:T(8,128)(2,1)S(1)}) custom-call(s32[1]{0:T(128)} %bitcast.6.chan_ref, s32[16]{0:T(128)} %keep_ref.1, f32[16,512,256]{2,1,0:T(8,128)} %records_ref.1, bf16[4,256,256]{2,1,0:T(8,128)(2,1)} %constant.22.clone.table_ref, f32[1,256]{1,0:T(1,128)} %constant.23.clone.taper_ref), custom_call_target="tpu_custom_call" | custom-call | flops 536870912 | bytes 11534336 | tf_op jit(solution)/shard_map/spectra_far/pallas_call | solution.py:87
  7.6 3.3 %collective-permute-start.6 = (bf16[4,16,4,16,128]{4,3,2,1,0:T(8,128)(2,1)S(1)}, bf16[4,16,4,16,128]{4,3,2,1,0:T(8,128)(2,1)S(1)}, u32[]{:S(2)}, u32[]{:S(2)}) collective-permute-start(bf16[4,16,4,16,128]{4,3,2,1,0:T(8,128)(2,1)S(1)} %get-tuple-element.102), channel_id=1, source_target_pairs={{0,1},{1,0},{2,3},{3,2},{4,5},{5,4},{6,7},{7,6},{8,9},{9,8},{10,11... | collective-permute-start | bytes 3145736 | tf_op jit(solution)/shard_map/ppermute | solution.py:359
  10.9 0.0 copy-done.2
  10.9 0.1 copy.14
  11.0 0.1 reshape.26.pairs_ref
  11.1 1.2 %couples.1 = s32[1]{0:T(128)} custom-call(s32[8]{0:T(128)S(1)} %reshape.26.pairs_ref), custom_call_target="tpu_custom_call" | custom-call | tf_op jit(solution)/shard_map/couples/pallas_call | solution.py:171
  12.9 0.1 pad_add_fusion
  13.0 0.2 collective-permute-done.6
  13.2 0.0 copy-done.1
  13.2 22.3 %conditional.1 = (bf16[16,4,2,4,16,128]{5,4,3,2,1,0:T(8,128)(2,1)}) conditional(s32[]{:T(128)} %bitcast.3, (s32[2]{0:T(128)S(1)}, s32[8]{0:T(128)S(1)}, bf16[4,16,4,16,128]{4,3,2,1,0:T(8,128)(2,1)S(1)}, bf16[4,16,4,16,128]{4,3,2,1,0:T(8,128)(2,1)S(1)}, s32[1]{0:T(128)}, /*index=5*/s32[16]{0:T(128)S(1)}, f32[16,512,256]{2,1,0:T(8,128)}, ...), branch_computations={%region_0.0_spmd, %region_1.0_spmd, %region_2.0_spmd} | conditional | flops 536870912 | bytes 34603096 | solution.py:389
  13.2 1.4 %sending.3 = (bf16[2,2,16,2,16,128]{5,4,3,2,1,0:T(8,128)(2,1)S(1)}, bf16[2,2,16,2,16,128]{5,4,3,2,1,0:T(8,128)(2,1)S(1)}) custom-call(s32[2]{0:T(128)S(1)} %get-tuple-element.62.place_ref, s32[8]{0:T(128)S(1)} %get-tuple-element.64.pairs_ref, bf16[4,16,4,16,128]{4,3,2,1,0:T(8,128)(2,1)S(1)} %get-tuple-element.65.mine_ref, ...), custom_call_target="tpu_custom_call" | custom-call | bytes 4194304 | tf_op jit(solution)/shard_map/cond/branch_0_fun/sending/pallas_call | solution.py:219
  14.6 3.9 %collective-permute-start.1 = (bf16[2,2,16,2,16,128]{5,4,3,2,1,0:T(8,128)(2,1)S(1)}, bf16[2,2,16,2,16,128]{5,4,3,2,1,0:T(8,128)(2,1)S(1)}, u32[]{:S(2)}, u32[]{:S(2)}) collective-permute-start(bf16[2,2,16,2,16,128]{5,4,3,2,1,0:T(8,128)(2,1)S(1)} %get-tuple-element.68), channel_id=1, source_target_pairs={{0,194},{2,64},{64,2},{66,128},{128,66},{130,192},{192,130},{194,0... | collective-permute-start | bytes 1572872 | tf_op jit(solution)/shard_map/cond/branch_0_fun/ppermute | solution.py:367
  18.6 0.0 collective-permute-start
  18.6 7.4 %spectra_near.3 = bf16[2,4,16,4,16,128]{5,4,3,2,1,0:T(8,128)(2,1)S(1)} custom-call(s32[1]{0:T(128)} %get-tuple-element.70.chan_ref, s32[16]{0:T(128)S(1)} %get-tuple-element.71.keep_ref, f32[16,512,256]{2,1,0:T(8,128)} %get-tuple-element.72.records_ref, bf16[4,256,256]{2,1,0:T(8,128)(2,1)} %get-tuple-element.73.table_ref, f32[1,256]{1,0:T(1,128)} %get-tuple-element.74.taper_ref), custom_call_target="tpu_custom_call" | custom-call | flops 536870912 | bytes 11534336 | tf_op jit(solution)/shard_map/cond/branch_0_fun/spectra_near/pallas_call | solution.py:87
  26.0 5.7 %all_to_all.22 = bf16[2,4,16,4,16,128]{5,4,3,2,1,0:T(8,128)(2,1)S(1)} all-to-all(bf16[2,4,16,4,16,128]{5,4,3,2,1,0:T(8,128)(2,1)S(1)} %spectra_near.3), channel_id=1, replica_groups=mesh['zh'=4,'y'=4,'x'=4,'zl'=2,'core'=2] {'core'}, dimensions={0} | all-to-all | bytes 4194304 | tf_op jit(solution)/shard_map/cond/branch_0_fun/all_to_all | solution.py:375
  31.7 1.7 %kept.3.kept_ref = bf16[16,4,2,4,16,128]{5,4,3,2,1,0:T(8,128)(2,1)} custom-call(s32[2]{0:T(128)S(1)} %get-tuple-element.62.place_ref, s32[8]{0:T(128)S(1)} %get-tuple-element.64.pairs_ref, bf16[8,16,4,16,128]{4,3,2,1,0:T(8,128)(2,1)S(1)} %bitcast.9), custom_call_target="tpu_custom_call" | custom-call | bytes 3145728 | tf_op jit(solution)/shard_map/cond/branch_0_fun/kept/pallas_call | solution.py:284
  33.4 0.0 collective-permute-done.1.outer_ref
  33.4 0.0 collective-permute-done.inner_ref
  33.4 1.8 %came.3 = bf16[16,4,2,4,16,128]{5,4,3,2,1,0:T(8,128)(2,1)} custom-call(s32[2]{0:T(128)S(1)} %get-tuple-element.62.place_ref, s32[8]{0:T(128)S(1)} %get-tuple-element.64.pairs_ref, bf16[2,2,16,2,16,128]{5,4,3,2,1,0:T(8,128)(2,1)S(1)} %collective-permute-done.inner_ref, ...), custom_call_target="tpu_custom_call", output_to_operand_aliasing={{}: (4, {})} | custom-call | bytes 3145728 | tf_op jit(solution)/shard_map/cond/branch_0_fun/came/pallas_call | solution.py:284
  35.5 34.3 %all_to_all.25.factors_ref = bf16[16,4,2,4,16,128]{5,4,3,2,1,0:T(8,128)(2,1)S(1)} all-to-all(bf16[16,4,2,4,16,128]{5,4,3,2,1,0:T(8,128)(2,1)} %get-tuple-element.103), channel_id=1, replica_groups=mesh['zh'=4,'y'=4,'x'=4,'zl'=2,'core'=2] {'y','x'}, dimensions={0} | all-to-all | bytes 4194304 | tf_op jit(solution)/shard_map/all_to_all | solution.py:394
  69.8 1.1 %products.1 = bf16[2048,128]{1,0:T(8,128)(2,1)S(1)} custom-call(bf16[16,4,2,4,16,128]{5,4,3,2,1,0:T(8,128)(2,1)S(1)} %all_to_all.25.factors_ref), custom_call_target="tpu_custom_call" | custom-call | flops 268435456 | bytes 3145728 | tf_op jit(solution)/shard_map/products/pallas_call | solution.py:318
  70.9 29.3 %all_to_all.26 = bf16[256,8,128]{2,1,0:T(8,128)(2,1)S(1)} all-to-all(bf16[256,8,128]{2,1,0:T(8,128)(2,1)S(1)} %bitcast.12), channel_id=1, replica_groups=mesh['zh'=4,'y'=4,'x'=4,'zl'=2,'core'=2] {'zh','y','x','zl','core'}, dimensions={0} | all-to-all | bytes 1048576 | tf_op jit(solution)/shard_map/all_to_all | solution.py:396
  100.2 0.0 copy-done
  100.2 1.1 %lags.1 = f32[1,256,512]{2,1,0:T(8,128)} custom-call(bf16[4,512,128]{2,1,0:T(8,128)(2,1)S(1)} %bitcast.13, bf16[2,512,512]{2,1,0:T(8,128)(2,1)S(1)} %copy-done), custom_call_target="tpu_custom_call" | custom-call | flops 134217728 | bytes 2097152 | tf_op jit(solution)/shard_map/lags/pallas_call | solution.py:347
  (3 shorter events, 0.0 us)
Async XLA Ops:
  0.0 10.9 %copy-start.2 = (s32[4,2]{0,1:T(2,128)S(1)}, s32[4,2]{0,1:T(2,128)}, u32[]{:S(2)}) copy-start(s32[4,2]{0,1:T(2,128)} %param.14) | copy-start | bytes 100
  0.0 13.2 %copy-start.1 = (s32[16]{0:T(128)S(1)}, s32[16]{0:T(128)}, u32[]{:S(2)}) copy-start(s32[16]{0:T(128)} %keep_ref.1) | copy-start | bytes 196
  7.6 5.6 %collective-permute-start.6 = (bf16[4,16,4,16,128]{4,3,2,1,0:T(8,128)(2,1)S(1)}, bf16[4,16,4,16,128]{4,3,2,1,0:T(8,128)(2,1)S(1)}, u32[]{:S(2)}, u32[]{:S(2)}) collective-permute-start(bf16[4,16,4,16,128]{4,3,2,1,0:T(8,128)(2,1)S(1)} %get-tuple-element.102), channel_id=1, source_target_pairs={{0,1},{1,0},{2,3},{3,2},{4,5},{5,4},{6,7},{7,6},{8,9},{9,8},{10,11... | collective-permute-start | bytes 3145736 | tf_op jit(solution)/shard_map/ppermute | solution.py:359
  14.6 18.8 %collective-permute-start.1 = (bf16[2,2,16,2,16,128]{5,4,3,2,1,0:T(8,128)(2,1)S(1)}, bf16[2,2,16,2,16,128]{5,4,3,2,1,0:T(8,128)(2,1)S(1)}, u32[]{:S(2)}, u32[]{:S(2)}) collective-permute-start(bf16[2,2,16,2,16,128]{5,4,3,2,1,0:T(8,128)(2,1)S(1)} %get-tuple-element.68), channel_id=1, source_target_pairs={{0,194},{2,64},{64,2},{66,128},{128,66},{130,192},{192,130},{194,0... | collective-permute-start | bytes 1572872 | tf_op jit(solution)/shard_map/cond/branch_0_fun/ppermute | solution.py:367
  18.6 14.8 %collective-permute-start = (bf16[2,2,16,2,16,128]{5,4,3,2,1,0:T(8,128)(2,1)S(1)}, bf16[2,2,16,2,16,128]{5,4,3,2,1,0:T(8,128)(2,1)S(1)}, u32[]{:S(2)}, u32[]{:S(2)}) collective-permute-start(bf16[2,2,16,2,16,128]{5,4,3,2,1,0:T(8,128)(2,1)S(1)} %get-tuple-element.67), channel_id=1, source_target_pairs={{0,2},{2,0},{1,3},{3,1},{4,6},{6,4},{5,7},{7,5},{8,10},{10,8},{9,1... | collective-permute-start | bytes 1572872 | tf_op jit(solution)/shard_map/cond/branch_0_fun/ppermute | solution.py:359
  69.8 30.4 %copy-start = (bf16[2,512,512]{2,1,0:T(8,128)(2,1)S(1)}, bf16[2,512,512]{2,1,0:T(8,128)(2,1)}, u32[]{:S(2)}) copy-start(bf16[2,512,512]{2,1,0:T(8,128)(2,1)} %constant.24.clone.refs_1_) | copy-start | bytes 3145732

commit v4 on v3

--- a/solution.py
+++ b/solution.py
@@ -56,7 +56,33 @@
     return both.reshape(-1, 2 * BINS, NFFT).astype(np.float32)
 
 
-def spectra_kernel(chan_ref, keep_ref, records_ref, table_ref, taper_ref, *refs):
+def named(step, chan_ref, pairs_ref):
+    marks = []
+    for k in range(OWN_BLKS):
+        block = chan_ref[0] * OWN_BLKS + k
+        mark = jnp.int32(0)
+        for p in range(NPAIR):
+            for side in range(2):
+                mark = jnp.where(pairs_ref[side, p] == block, 1, mark)
+        marks.append(mark)
+    count = sum(marks[1:], marks[0])
+    want = jnp.minimum(step, jnp.maximum(count - 1, 0))
+    at, seen = jnp.int32(0), jnp.int32(0)
+    for k, mark in enumerate(marks):
+        at = jnp.where((mark == 1) & (seen == want), k, at)
+        seen = seen + mark
+    return at, step < count
+
+
+def spectra_kernel(chan_ref, keep_ref, pairs_ref, *refs):
+    there = named(pl.program_id(0), chan_ref, pairs_ref)[1]
+
+    @pl.when(there)
+    def _():
+        block_spectra(keep_ref, *refs)
+
+
+def block_spectra(keep_ref, records_ref, table_ref, taper_ref, *refs):
     outs, rows_ref = refs[:-1], refs[-1]
     table = table_ref[0]
     taper = taper_ref[...]
@@ -78,20 +104,22 @@
     return pltpu.with_memory_space_constraint(x, pltpu.HBM)
 
 
-def spectra(half, lead, count, name, chan, keep, records, tables):
+def spectra(half, lead, count, name, chan, keep, pairs, records, tables):
     steps = np.arange(SEG, dtype=np.float64)
     taper = jnp.asarray((0.5 - 0.5 * np.cos(2.0 * math.pi * (steps + 0.5) / SEG)).astype(np.float32)[None])
     tail = (YX, 2 * BINS, OWN_SEGS, BLK)
     out = jax.ShapeDtypeStruct(lead + (OWN_BLKS,) + tail, BF16)
-    out_spec = pl.BlockSpec(lead + (1,) + tail, lambda b, *_: (0,) * len(lead) + (b, 0, 0, 0, 0))
+    out_spec = pl.BlockSpec(
+        lead + (1,) + tail, lambda b, c, k, q: (0,) * len(lead) + (named(b, c, q)[0], 0, 0, 0, 0)
+    )
     return pl.pallas_call(
         spectra_kernel,
         grid_spec=pltpu.PrefetchScalarGridSpec(
-            num_scalar_prefetch=2,
+            num_scalar_prefetch=3,
             grid=(OWN_BLKS,),
             in_specs=[
-                pl.BlockSpec((OWN_SEGS, BLK, SEG), lambda b, *_: (0, b, 0)),
-                pl.BlockSpec((1, NBAND, SEG), lambda b, c, k: (c[0], half, 0)),
+                pl.BlockSpec((OWN_SEGS, BLK, SEG), lambda b, c, k, q: (0, named(b, c, q)[0], 0)),
+                pl.BlockSpec((1, NBAND, SEG), lambda b, c, k, q: (c[0], half, 0)),
                 pl.BlockSpec((1, SEG), lambda b, *_: (0, 0)),
             ],
             out_specs=[out_spec] * count,
@@ -101,7 +129,7 @@
         compiler_params=pltpu.CompilerParams(vmem_limit_bytes=16 * MIB),
         cost_estimate=pl.CostEstimate(flops=8192 * 256 * 256, bytes_accessed=11 * MIB, transcendentals=8192),
         name=name,
-    )(chan, keep, in_hbm(records), in_hbm(tables), in_hbm(taper))
+    )(chan, keep, pairs, in_hbm(records), in_hbm(tables), in_hbm(taper))
 
 
 def whose(block, zl, core):
@@ -138,7 +166,7 @@
     flags = []
     alone, doubles = jnp.int32(0), jnp.int32(0)
     for p in range(NPAIR):
-        a, b = (pairs[2 * p + side] // (CORE * OWN_BLKS) == zl for side in range(2))
+        a, b = (pairs[side, p] // (CORE * OWN_BLKS) == zl for side in range(2))
         one, both = jnp.where(a != b, 1, 0), jnp.where(a & b, 1, 0)
         flags.append((one, both))
         alone, doubles = alone + one, doubles + 2 * both
@@ -182,7 +210,7 @@
     plan = crossing(pairs_ref, zl)[2]
     for start in (True, False):
         for p in range(NPAIR):
-            blocks = (pairs_ref[2 * p], pairs_ref[2 * p + 1])
+            blocks = (pairs_ref[0, p], pairs_ref[1, p])
             one, at, both, bins = plan[p]
             here_a = whose(blocks[0], zl, core)[0]
             lone = jnp.where(here_a, blocks[0], blocks[1])
@@ -231,7 +259,7 @@
 def places(pairs_ref, zl, core):
     for p in range(NPAIR):
         for side in range(2):
-            block = pairs_ref[2 * p + side]
+            block = pairs_ref[side, p]
             for bin_ in range(BINS):
                 yield (2 * p + side) * BINS + bin_, p, side, bin_, block, whose(block, zl, core)[0]
 
@@ -371,7 +399,7 @@
     inner, outer = sending(couples, place, pairs, mine_far, other_far)
     later, *_ = lax.optimization_barrier((chan, inner))
     inner, outer = swap(inner, "zl"), swap_outer(outer)
-    (chip,) = spectra(0, (CORE,), 1, "spectra_near", later, keep, records, tables)
+    (chip,) = spectra(0, (CORE,), 1, "spectra_near", later, keep, pairs, records, tables)
     chip = lax.all_to_all(chip, "core", 0, 0, tiled=True)
     chip = chip.reshape((CORE * OWN_BLKS,) + chip.shape[2:])
     kept = sides_of(kept_kernel, "kept", place, pairs, chip)
@@ -382,14 +410,14 @@
     zl, core = lax.axis_index("zl"), lax.axis_index("core")
     place = jnp.stack([zl, core]).astype(jnp.int32)
     chan = (zl * CORE + core).astype(jnp.int32).reshape(1)
-    flat = pairs.reshape(-1)
+    sides_first = pairs.T
     tables = jnp.asarray(forward_tables(), BF16)
-    mine_far, theirs_far = spectra(1, (), 2, "spectra_far", chan, keep, records, tables)
+    mine_far, theirs_far = spectra(1, (), 2, "spectra_far", chan, keep, sides_first, records, tables)
     other_far = swap(theirs_far, "core")
     sides = lax.switch(
-        couples_of(flat) - LEAST,
+        couples_of(sides_first) - LEAST,
         [functools.partial(both_sides, couples) for couples in range(LEAST, NPAIR + 1)],
-        *(place, flat, chan, keep, records, tables, mine_far, other_far),
+        *(place, sides_first, chan, keep, records, tables, mine_far, other_far),
     )
     gathered = lax.all_to_all(sides, ("y", "x"), 0, 0, tiled=True)
     shares = products(gathered).reshape(ZH * YX * NPAIR, 8, BLK)

time: 103 us -> 98.4 us (0.955)
  Pallas kernels: 23.3 us -> 16.3 us
  starting transfers between devices: 7.25 us -> 8.41 us
    pallas_call x2, Pallas kernels: 15 us -> 7.93 us  [spectra(): pl.pallas_call(spectra_kernel, grid_spec=pltpu.PrefetchScalarGridSpec(num...]
    all_to_all x1, blocking collectives: 5.69 us -> 6.91 us  [both_sides(): chip = lax.all_to_all(chip, 'core', 0, 0, tiled=True)]
    ppermute x2, starting transfers between devices: 3.33 us -> 4.49 us  [swap(): return lax.ppermute(x, axis, [(0, 1), (1, 0)])]
  transfers between devices with their start and end apart: 3 -> 3, of which waited for: 1 -> 2; matrix products, arithmetic and copies ran while one was open for 0% -> 0% of each run, Pallas kernels for 10% -> 7%
where the time goes in v4:
time: 98.4 us; the launch traced here: 96.7 us
  blocking collectives  70.3 us (71%)
  Pallas kernels  16.3 us (17%)
  starting transfers between devices  8.41 us (9%)
    all_to_all x1, blocking collectives, shards(): gathered = lax.all_to_all(sides, ('y', 'x'), 0, 0, tiled=True)  33.6 us
    all_to_all x1, blocking collectives, shards(): lax.all_to_all(shares, ('zh', 'y', 'x', 'zl', 'core'), 0, 0, tiled=True)  29.8 us
    pallas_call x2, Pallas kernels, spectra(): pl.pallas_call(spectra_kernel, grid_spec=pltpu.PrefetchScalarGridSpec(num...  7.93 us
    all_to_all x1, blocking collectives, both_sides(): chip = lax.all_to_all(chip, 'core', 0, 0, tiled=True)  6.91 us
    ppermute x2, starting transfers between devices, swap(): return lax.ppermute(x, axis, [(0, 1), (1, 0)])  4.49 us
    ppermute x1, starting transfers between devices, swap_outer(): return lax.ppermute(x, ('zh', 'zl'), turns)  3.92 us
    pallas_call x2, Pallas kernels, sides_of(): pl.pallas_call(kernel, in_specs=[smem(), smem()] + [hbm()] * len(arrays),...  3.53 us
  transfers between devices with their start and end apart: 3, of which 2 were waited for; matrix products, arithmetic and copies ran while one was open for 0% of the time, Pallas kernels for 7%

profile of v4, /device:TPU:1, one launch (start us, length us, event | category | flops | bytes accessed | tf_op | source)
XLA Modules:
  0.0 96.7 jit_solution(14496277445217258615)
XLA Ops:
  0.0 0.0 copy-start.1
  0.0 0.0 copy-start.2
  0.0 4.1 %spectra_far.1 = (bf16[4,16,4,16,128]{4,3,2,1,0:T(8,128)(2,1)S(1)}, bf16[4,16,4,16,128]{4,3,2,1,0:T(8,128)(2,1)S(1)}) custom-call(s32[1]{0:T(128)} %bitcast.7.chan_ref, s32[16]{0:T(128)} %keep_ref.1, s32[2,4]{1,0:T(2,128)} %bitcast.15, f32[16,512,256]{2,1,0:T(8,128)} %refs_0_.1, bf16[4,256,256]{2,1,0:T(8,128)(2,1)} %constant.22.clone.refs_1_, ...), custom_call_target="tpu_custom_call" | custom-call | flops 536870912 | bytes 11534336 | tf_op jit(solution)/shard_map/spectra_far/pallas_call | solution.py:115
  4.1 4.5 %collective-permute-start.6 = (bf16[4,16,4,16,128]{4,3,2,1,0:T(8,128)(2,1)S(1)}, bf16[4,16,4,16,128]{4,3,2,1,0:T(8,128)(2,1)S(1)}, u32[]{:S(2)}, u32[]{:S(2)}) collective-permute-start(bf16[4,16,4,16,128]{4,3,2,1,0:T(8,128)(2,1)S(1)} %get-tuple-element.102), channel_id=1, source_target_pairs={{0,1},{1,0},{2,3},{3,2},{4,5},{5,4},{6,7},{7,6},{8,9},{9,8},{10,11... | collective-permute-start | bytes 3145736 | tf_op jit(solution)/shard_map/ppermute | solution.py:387
  8.6 0.0 copy-done.1
  8.6 1.2 %couples.1 = s32[1]{0:T(128)} custom-call(s32[2,4]{1,0:T(2,128)S(1)} %bitcast.16), custom_call_target="tpu_custom_call" | custom-call | tf_op jit(solution)/shard_map/couples/pallas_call | solution.py:199
  10.4 0.1 pad_add_fusion
  10.5 0.4 collective-permute-done.6
  10.8 0.0 copy-done.2
  10.8 20.2 %conditional.1 = (bf16[16,4,2,4,16,128]{5,4,3,2,1,0:T(8,128)(2,1)}) conditional(s32[]{:T(128)} %bitcast.4, (s32[2]{0:T(128)S(1)}, s32[2,4]{1,0:T(2,128)S(1)}, bf16[4,16,4,16,128]{4,3,2,1,0:T(8,128)(2,1)S(1)}, bf16[4,16,4,16,128]{4,3,2,1,0:T(8,128)(2,1)S(1)}, s32[1]{0:T(128)}, /*index=5*/s32[16]{0:T(128)S(1)}, ...), branch_computations={%region_0.0_spmd, %region_1.0_spmd, %region_2.0_spmd} | conditional | flops 536870912 | bytes 34603096 | solution.py:417
  10.8 1.4 %sending.3 = (bf16[2,2,16,2,16,128]{5,4,3,2,1,0:T(8,128)(2,1)S(1)}, bf16[2,2,16,2,16,128]{5,4,3,2,1,0:T(8,128)(2,1)S(1)}) custom-call(s32[2]{0:T(128)S(1)} %get-tuple-element.62.place_ref, s32[2,4]{1,0:T(2,128)S(1)} %get-tuple-element.64.pairs_ref, bf16[4,16,4,16,128]{4,3,2,1,0:T(8,128)(2,1)S(1)} %get-tuple-element.65.mine_ref, ...), custom_call_target="tpu_custom_call" | custom-call | bytes 4194304 | tf_op jit(solution)/shard_map/cond/branch_0_fun/sending/pallas_call | solution.py:247
  12.3 3.9 %collective-permute-start.1 = (bf16[2,2,16,2,16,128]{5,4,3,2,1,0:T(8,128)(2,1)S(1)}, bf16[2,2,16,2,16,128]{5,4,3,2,1,0:T(8,128)(2,1)S(1)}, u32[]{:S(2)}, u32[]{:S(2)}) collective-permute-start(bf16[2,2,16,2,16,128]{5,4,3,2,1,0:T(8,128)(2,1)S(1)} %get-tuple-element.68), channel_id=1, source_target_pairs={{0,194},{2,64},{64,2},{66,128},{128,66},{130,192},{192,130},{194,0... | collective-permute-start | bytes 1572872 | tf_op jit(solution)/shard_map/cond/branch_0_fun/ppermute | solution.py:395
  16.2 0.0 collective-permute-start
  16.2 3.9 %spectra_near.3 = bf16[2,4,16,4,16,128]{5,4,3,2,1,0:T(8,128)(2,1)S(1)} custom-call(s32[1]{0:T(128)} %get-tuple-element.70.chan_ref, s32[16]{0:T(128)S(1)} %get-tuple-element.71.keep_ref, s32[2,4]{1,0:T(2,128)S(1)} %get-tuple-element.64.pairs_ref, f32[16,512,256]{2,1,0:T(8,128)} %get-tuple-element.72.refs_0_, bf16[4,256,256]{2,1,0:T(8,128)(2,1)} %get-tuple-element.73.refs_1_, ...), custom_call_target="tpu_custom_call" | custom-call | flops 536870912 | bytes 11534336 | tf_op jit(solution)/shard_map/cond/branch_0_fun/spectra_near/pallas_call | solution.py:115
  20.1 6.9 %all_to_all.22 = bf16[2,4,16,4,16,128]{5,4,3,2,1,0:T(8,128)(2,1)S(1)} all-to-all(bf16[2,4,16,4,16,128]{5,4,3,2,1,0:T(8,128)(2,1)S(1)} %spectra_near.3), channel_id=1, replica_groups=mesh['zh'=4,'y'=4,'x'=4,'zl'=2,'core'=2] {'core'}, dimensions={0} | all-to-all | bytes 4194304 | tf_op jit(solution)/shard_map/cond/branch_0_fun/all_to_all | solution.py:403
  27.0 1.7 %kept.3.kept_ref = bf16[16,4,2,4,16,128]{5,4,3,2,1,0:T(8,128)(2,1)} custom-call(s32[2]{0:T(128)S(1)} %get-tuple-element.62.place_ref, s32[2,4]{1,0:T(2,128)S(1)} %get-tuple-element.64.pairs_ref, bf16[8,16,4,16,128]{4,3,2,1,0:T(8,128)(2,1)S(1)} %bitcast.10), custom_call_target="tpu_custom_call" | custom-call | bytes 3145728 | tf_op jit(solution)/shard_map/cond/branch_0_fun/kept/pallas_call | solution.py:312
  28.7 0.0 collective-permute-done.1.outer_ref
  28.7 0.3 collective-permute-done.inner_ref
  29.0 1.8 %came.3 = bf16[16,4,2,4,16,128]{5,4,3,2,1,0:T(8,128)(2,1)} custom-call(s32[2]{0:T(128)S(1)} %get-tuple-element.62.place_ref, s32[2,4]{1,0:T(2,128)S(1)} %get-tuple-element.64.pairs_ref, bf16[2,2,16,2,16,128]{5,4,3,2,1,0:T(8,128)(2,1)S(1)} %collective-permute-done.inner_ref, ...), custom_call_target="tpu_custom_call", output_to_operand_aliasing={{}: (4, {})} | custom-call | bytes 3145728 | tf_op jit(solution)/shard_map/cond/branch_0_fun/came/pallas_call | solution.py:312
  31.1 33.6 %all_to_all.25.factors_ref = bf16[16,4,2,4,16,128]{5,4,3,2,1,0:T(8,128)(2,1)S(1)} all-to-all(bf16[16,4,2,4,16,128]{5,4,3,2,1,0:T(8,128)(2,1)} %get-tuple-element.103), channel_id=1, replica_groups=mesh['zh'=4,'y'=4,'x'=4,'zl'=2,'core'=2] {'y','x'}, dimensions={0} | all-to-all | bytes 4194304 | tf_op jit(solution)/shard_map/all_to_all | solution.py:422
  64.7 1.1 %products.1 = bf16[2048,128]{1,0:T(8,128)(2,1)S(1)} custom-call(bf16[16,4,2,4,16,128]{5,4,3,2,1,0:T(8,128)(2,1)S(1)} %all_to_all.25.factors_ref), custom_call_target="tpu_custom_call" | custom-call | flops 268435456 | bytes 3145728 | tf_op jit(solution)/shard_map/products/pallas_call | solution.py:346
  65.7 29.8 %all_to_all.26 = bf16[256,8,128]{2,1,0:T(8,128)(2,1)S(1)} all-to-all(bf16[256,8,128]{2,1,0:T(8,128)(2,1)S(1)} %bitcast.13), channel_id=1, replica_groups=mesh['zh'=4,'y'=4,'x'=4,'zl'=2,'core'=2] {'zh','y','x','zl','core'}, dimensions={0} | all-to-all | bytes 1048576 | tf_op jit(solution)/shard_map/all_to_all | solution.py:424
  95.6 0.0 copy-done
  95.6 1.1 %lags.1 = f32[1,256,512]{2,1,0:T(8,128)} custom-call(bf16[4,512,128]{2,1,0:T(8,128)(2,1)S(1)} %bitcast.14, bf16[2,512,512]{2,1,0:T(8,128)(2,1)S(1)} %copy-done), custom_call_target="tpu_custom_call" | custom-call | flops 134217728 | bytes 2097152 | tf_op jit(solution)/shard_map/lags/pallas_call | solution.py:375
  (1 shorter events, 0.0 us)
Async XLA Ops:
  0.0 8.6 %copy-start.1 = (s32[4,2]{0,1:T(2,128)S(1)}, s32[4,2]{0,1:T(2,128)}, u32[]{:S(2)}) copy-start(s32[4,2]{0,1:T(2,128)} %param.14) | copy-start | bytes 100
  0.0 10.8 %copy-start.2 = (s32[16]{0:T(128)S(1)}, s32[16]{0:T(128)}, u32[]{:S(2)}) copy-start(s32[16]{0:T(128)} %keep_ref.1) | copy-start | bytes 196
  4.1 6.8 %collective-permute-start.6 = (bf16[4,16,4,16,128]{4,3,2,1,0:T(8,128)(2,1)S(1)}, bf16[4,16,4,16,128]{4,3,2,1,0:T(8,128)(2,1)S(1)}, u32[]{:S(2)}, u32[]{:S(2)}) collective-permute-start(bf16[4,16,4,16,128]{4,3,2,1,0:T(8,128)(2,1)S(1)} %get-tuple-element.102), channel_id=1, source_target_pairs={{0,1},{1,0},{2,3},{3,2},{4,5},{5,4},{6,7},{7,6},{8,9},{9,8},{10,11... | collective-permute-start | bytes 3145736 | tf_op jit(solution)/shard_map/ppermute | solution.py:387
  12.3 16.4 %collective-permute-start.1 = (bf16[2,2,16,2,16,128]{5,4,3,2,1,0:T(8,128)(2,1)S(1)}, bf16[2,2,16,2,16,128]{5,4,3,2,1,0:T(8,128)(2,1)S(1)}, u32[]{:S(2)}, u32[]{:S(2)}) collective-permute-start(bf16[2,2,16,2,16,128]{5,4,3,2,1,0:T(8,128)(2,1)S(1)} %get-tuple-element.68), channel_id=1, source_target_pairs={{0,194},{2,64},{64,2},{66,128},{128,66},{130,192},{192,130},{194,0... | collective-permute-start | bytes 1572872 | tf_op jit(solution)/shard_map/cond/branch_0_fun/ppermute | solution.py:395
  16.2 12.8 %collective-permute-start = (bf16[2,2,16,2,16,128]{5,4,3,2,1,0:T(8,128)(2,1)S(1)}, bf16[2,2,16,2,16,128]{5,4,3,2,1,0:T(8,128)(2,1)S(1)}, u32[]{:S(2)}, u32[]{:S(2)}) collective-permute-start(bf16[2,2,16,2,16,128]{5,4,3,2,1,0:T(8,128)(2,1)S(1)} %get-tuple-element.67), channel_id=1, source_target_pairs={{0,2},{2,0},{1,3},{3,1},{4,6},{6,4},{5,7},{7,5},{8,10},{10,8},{9,1... | collective-permute-start | bytes 1572872 | tf_op jit(solution)/shard_map/cond/branch_0_fun/ppermute | solution.py:387
  64.7 30.9 %copy-start = (bf16[2,512,512]{2,1,0:T(8,128)(2,1)S(1)}, bf16[2,512,512]{2,1,0:T(8,128)(2,1)}, u32[]{:S(2)}) copy-start(bf16[2,512,512]{2,1,0:T(8,128)(2,1)} %constant.24.clone.refs_1_) | copy-start | bytes 3145732
